TPU v7x, 32 devices: a whole 2x2x4 slice. The times are simulated.
32 devices in a mesh: dp: 2 (over x), row: 4 (over y, core), col: 4 (over z).
Axes of the slice: x: 2, y: 2, z: 4, core: 2. Of those that a mesh axis runs over, the one named last changes fastest.
Arguments:
- tokens: bfloat16 [8192, 1024], P(('dp', 'col'), 'row'), may hold values from -6 to 6
- segments: int32 [16, 512], P(('dp', 'row')), may hold values from 0 to 7, never falling along the last dimension, each value on 1 to 256 neighbouring positions
- qkv_weight: bfloat16 [1024, 3, 1024], P('row', None, 'col'), may hold values from -0.1875 to 0.1875
- qv_bias: float32 [2, 1024], P(None, 'col'), may hold values from -3 to 3
- out_weight: bfloat16 [1024, 1024], P('col', 'row'), may hold values from -0.75 to 0.75
- out_bias: float32 [1024], replicated, may hold values from -3 to 3
- norm1_gain: float32 [1024], replicated, may hold values from 0.5 to 1.5
- norm1_bias: float32 [1024], replicated, may hold values from -3 to 3
- up_weight: bfloat16 [1024, 4096], P('row', 'col'), may hold values from -0.1875 to 0.1875
- up_bias: float32 [4096], P('col'), may hold values from -3 to 3
- down_weight: bfloat16 [4096, 1024], P('col', 'row'), may hold values from -0.09375 to 0.09375
- down_bias: float32 [1024], replicated, may hold values from -3 to 3
- norm2_gain: float32 [1024], replicated, may hold values from 0.5 to 1.5
- norm2_bias: float32 [1024], replicated, may hold values from -3 to 3
- out_grad: bfloat16 [8192, 1024], P(('dp', 'col'), 'row'), may hold values from -6 to 6
Outputs:
- layer_out: bfloat16 [8192, 1024], P(('dp', 'col'), 'row')
- tokens_grad: float32 [8192, 1024], P(('dp', 'col'), 'row')
- qkv_weight_grad: float32 [1024, 3, 1024], P('row', None, 'col')
- qv_bias_grad: float32 [2, 1024], P(None, 'col')
- out_weight_grad: float32 [1024, 1024], P('col', 'row')
- out_bias_grad: float32 [1024], P('row')
- norm1_gain_grad: float32 [1024], P('row')
- norm1_bias_grad: float32 [1024], P('row')
- up_weight_grad: float32 [1024, 4096], P('row', 'col')
- up_bias_grad: float32 [4096], P('col')
- down_weight_grad: float32 [4096, 1024], P('col', 'row')
- down_bias_grad: float32 [1024], P('row')
- norm2_gain_grad: float32 [1024], P('row')
- norm2_bias_grad: float32 [1024], P('row')
Inputs may be any that keep to these rules, and one draw needn't show every extreme that they name: `segments`: within each sequence the document numbers never fall; each document covers 1 to 256 tokens, and one of each draw covers exactly 256.
All inputs are finite; a program needn't handle non-finite values.
Results may differ from a plain program's by a relative error of at most 0.014.
Values may be sent and summed in bfloat16 or wider, within the bound.
A program may use at most 128 MiB of HBM per device.

v0:
```python
import jax
import jax.numpy as jnp
from jax import lax
from jax.sharding import PartitionSpec as P

D = 1024
HEAD = 64
SEQ = 512


EPS = 1e-05


def col_gather(values):
    return lax.all_gather(values, "col", axis=0, tiled=True)


def row_gather(values):
    return lax.all_gather(values, "row", axis=0, tiled=True)


def row_product(gathered, weight, contract):
    return lax.psum_scatter(
        lax.dot_general(
            gathered, weight, (((1,), (contract,)), ((), ())), preferred_element_type=jnp.float32
        ),
        "row",
        scatter_dimension=0,
        tiled=True,
    )


def col_product(gathered, weight, contract):
    return lax.psum_scatter(
        lax.dot_general(
            gathered, weight, (((1,), (contract,)), ((), ())), preferred_element_type=jnp.float32
        ),
        "col",
        scatter_dimension=0,
        tiled=True,
    )


def contract_rows(left, right):
    return lax.dot_general(
        left, right, (((0,), (0,)), ((), ())), preferred_element_type=jnp.float32
    )


def row_stats(first_part, second_part):
    return lax.psum((first_part, second_part), "row")


def norm_forward(summed, gain, offset, stats):
    total, squares = stats(jnp.sum(summed, 1), jnp.sum(summed * summed, 1))
    center = total / D
    spread = squares / D - center * center
    inverse = lax.rsqrt(spread + EPS)
    normed = (summed - center[:, None]) * inverse[:, None]
    return (normed * gain + offset, normed, inverse)


def norm_backward(grad_norm, normed, inverse, gain, stats):
    scaled = grad_norm * gain
    first_mean, second_mean = stats(jnp.sum(scaled, 1), jnp.sum(scaled * normed, 1))
    return inverse[:, None] * (scaled - first_mean[:, None] / D - normed * second_mean[:, None] / D)


def gelu_exact(values):
    return jax.nn.gelu(values, approximate=False)


def masked_scores(queries, keys_in, labels):
    scale_factor = float(HEAD) ** (-0.5)
    scores = (
        jnp.einsum("qhe,khe->hqk", queries, keys_in, preferred_element_type=jnp.float32)
        * scale_factor
    )
    same_doc = labels[:, None] == labels[None, :]
    return jnp.where(same_doc[None], scores, -1e30)


def attend_forward(packed):
    queries, keys_in, values_in, labels = packed
    scores = masked_scores(queries, keys_in, labels)
    highest = jnp.max(scores, -1, keepdims=True)
    weights = jnp.exp(scores - highest)
    totals = jnp.sum(weights, -1, keepdims=True)
    probs = (weights / totals).astype(jnp.bfloat16)
    context = jnp.einsum("hqk,khe->qhe", probs, values_in, preferred_element_type=jnp.float32)
    return (context, highest[..., 0] + jnp.log(totals[..., 0]))


def attend_backward(packed):
    queries, keys_in, values_in, labels, logsum, grad_context = packed
    scale_factor = float(HEAD) ** (-0.5)
    scores = masked_scores(queries, keys_in, labels)
    probs = jnp.exp(scores - logsum[..., None])
    grad_probs = jnp.einsum(
        "qhe,khe->hqk", grad_context, values_in, preferred_element_type=jnp.float32
    )
    weighted = jnp.sum(grad_probs * probs, -1, keepdims=True)
    grad_scores = (probs * (grad_probs - weighted)).astype(jnp.bfloat16)
    grad_queries = (
        jnp.einsum("hqk,khe->qhe", grad_scores, keys_in, preferred_element_type=jnp.float32)
        * scale_factor
    )
    grad_keys = (
        jnp.einsum("hqk,qhe->khe", grad_scores, queries, preferred_element_type=jnp.float32)
        * scale_factor
    )
    grad_values = jnp.einsum(
        "hqk,qhe->khe", probs.astype(jnp.bfloat16), grad_context, preferred_element_type=jnp.float32
    )
    return jnp.stack([grad_queries, grad_keys, grad_values], 1)


def attention_block(projected, segments, seqs_local, heads_local):
    projected = projected.reshape(seqs_local, SEQ, 3, heads_local, HEAD)
    queries = projected[:, :, 0]
    keys_all = projected[:, :, 1]
    values_all = projected[:, :, 2]
    context, logsum = lax.map(attend_forward, (queries, keys_all, values_all, segments))
    return (queries, keys_all, values_all, context, logsum)


def grid_plan(
    tokens,
    segments,
    qkv_weight,
    qv_bias,
    out_weight,
    out_bias,
    norm1_gain,
    norm1_bias,
    up_weight,
    up_bias,
    down_weight,
    down_bias,
    norm2_gain,
    norm2_bias,
    out_grad,
):
    tok_local = tokens.shape[0]
    part_width = tokens.shape[1]
    head_width = qkv_weight.shape[2]
    heads_local = head_width // HEAD
    seqs_local = segments.shape[0]
    row_place = lax.axis_index("row") * part_width

    def own_part(vector):
        return lax.dynamic_slice_in_dim(vector, row_place, part_width)

    qkv_flat = qkv_weight.reshape(part_width, 3 * head_width)
    bias_rows = jnp.stack([qv_bias[0], jnp.zeros_like(qv_bias[0]), qv_bias[1]]).reshape(
        1, 3 * head_width
    )
    gathered_x = col_gather(tokens)
    projected = (row_product(gathered_x, qkv_flat, 0) + bias_rows).astype(jnp.bfloat16)
    queries, keys_all, values_all, context, logsum = attention_block(
        projected, segments, seqs_local, heads_local
    )
    context_b = context.reshape(tok_local, head_width).astype(jnp.bfloat16)
    gathered_ctx = row_gather(context_b)
    attended = col_product(gathered_ctx, out_weight, 0) + own_part(out_bias)
    first_sum = tokens.astype(jnp.float32) + attended
    hidden, normed1, inverse1 = norm_forward(
        first_sum, own_part(norm1_gain), own_part(norm1_bias), row_stats
    )
    hidden_b = hidden.astype(jnp.bfloat16)
    gathered_h = col_gather(hidden_b)
    upward = row_product(gathered_h, up_weight, 0) + up_bias
    activated, gelu_pull = jax.vjp(gelu_exact, upward)
    activated_b = activated.astype(jnp.bfloat16)
    gathered_a = row_gather(activated_b)
    downward = col_product(gathered_a, down_weight, 0) + own_part(down_bias)
    second_sum = hidden + downward
    layer_out, normed2, inverse2 = norm_forward(
        second_sum, own_part(norm2_gain), own_part(norm2_bias), row_stats
    )
    grad_layer = out_grad.astype(jnp.float32)
    norm2_gain_part = jnp.sum(grad_layer * normed2, 0)
    norm2_bias_part = jnp.sum(grad_layer, 0)
    grad_second = norm_backward(grad_layer, normed2, inverse2, own_part(norm2_gain), row_stats)
    grad_down_g = col_gather(grad_second.astype(jnp.bfloat16))
    down_weight_grad = contract_rows(gathered_a, grad_down_g)
    down_bias_grad = jnp.sum(grad_down_g.astype(jnp.float32), 0)
    grad_activated = row_product(grad_down_g, down_weight, 1)
    (grad_upward,) = gelu_pull(grad_activated)
    grad_up_g = row_gather(grad_upward.astype(jnp.bfloat16))
    up_weight_grad = contract_rows(gathered_h, grad_up_g)
    up_bias_grad = jnp.sum(grad_up_g.astype(jnp.float32), 0)
    grad_hidden = grad_second + col_product(grad_up_g, up_weight, 1)
    norm1_gain_part = jnp.sum(grad_hidden * normed1, 0)
    norm1_bias_part = jnp.sum(grad_hidden, 0)
    grad_first = norm_backward(grad_hidden, normed1, inverse1, own_part(norm1_gain), row_stats)
    grad_attn_g = col_gather(grad_first.astype(jnp.bfloat16))
    out_weight_grad = contract_rows(gathered_ctx, grad_attn_g)
    out_bias_grad = jnp.sum(grad_attn_g.astype(jnp.float32), 0)
    grad_context = row_product(grad_attn_g, out_weight, 1).astype(jnp.bfloat16)
    grad_context = grad_context.reshape(seqs_local, SEQ, heads_local, HEAD)
    grad_projected = lax.map(
        attend_backward, (queries, keys_all, values_all, segments, logsum, grad_context)
    )
    grad_proj_g = row_gather(grad_projected.reshape(tok_local, 3 * head_width).astype(jnp.bfloat16))
    qkv_weight_grad = contract_rows(gathered_x, grad_proj_g).reshape(part_width, 3, head_width)
    bias_sums = jnp.sum(grad_proj_g.astype(jnp.float32), 0).reshape(3, head_width)
    qv_bias_grad = jnp.stack([bias_sums[0], bias_sums[2]])
    tokens_grad = grad_first + col_product(grad_proj_g, qkv_flat, 1)
    return (
        layer_out.astype(jnp.bfloat16),
        tokens_grad,
        qkv_weight_grad,
        qv_bias_grad,
        out_weight_grad,
        out_bias_grad,
        norm1_gain_part,
        norm1_bias_part,
        up_weight_grad,
        up_bias_grad,
        down_weight_grad,
        down_bias_grad,
        norm2_gain_part,
        norm2_bias_part,
    )


def shards(
    tokens,
    segments,
    qkv_weight,
    qv_bias,
    out_weight,
    out_bias,
    norm1_gain,
    norm1_bias,
    up_weight,
    up_bias,
    down_weight,
    down_bias,
    norm2_gain,
    norm2_bias,
    out_grad,
):
    arguments = (
        tokens,
        segments,
        qkv_weight,
        qv_bias,
        out_weight,
        out_bias,
        norm1_gain,
        norm1_bias,
        up_weight,
        up_bias,
        down_weight,
        down_bias,
        norm2_gain,
        norm2_bias,
        out_grad,
    )
    results = grid_plan(*arguments)
    (
        layer_out,
        tokens_grad,
        qkv_weight_grad,
        qv_bias_grad,
        out_weight_grad,
        out_bias_grad,
        norm1_gain_part,
        norm1_bias_part,
        up_weight_grad,
        up_bias_grad,
        down_weight_grad,
        down_bias_grad,
        norm2_gain_part,
        norm2_bias_part,
    ) = results
    norm1_gain_grad, norm1_bias_grad, norm2_gain_grad, norm2_bias_grad = lax.psum(
        (norm1_gain_part, norm1_bias_part, norm2_gain_part, norm2_bias_part), ("dp", "col")
    )
    (
        qkv_weight_grad,
        qv_bias_grad,
        out_weight_grad,
        out_bias_grad,
        up_weight_grad,
        up_bias_grad,
        down_weight_grad,
        down_bias_grad,
    ) = (
        lax.psum(qkv_weight_grad.astype(jnp.bfloat16), "dp").astype(jnp.float32),
        lax.psum(qv_bias_grad.astype(jnp.bfloat16), "dp").astype(jnp.float32),
        lax.psum(out_weight_grad.astype(jnp.bfloat16), "dp").astype(jnp.float32),
        lax.psum(out_bias_grad.astype(jnp.bfloat16), "dp").astype(jnp.float32),
        lax.psum(up_weight_grad.astype(jnp.bfloat16), "dp").astype(jnp.float32),
        lax.psum(up_bias_grad.astype(jnp.bfloat16), "dp").astype(jnp.float32),
        lax.psum(down_weight_grad.astype(jnp.bfloat16), "dp").astype(jnp.float32),
        lax.psum(down_bias_grad.astype(jnp.bfloat16), "dp").astype(jnp.float32),
    )
    return (
        layer_out,
        tokens_grad,
        qkv_weight_grad,
        qv_bias_grad,
        out_weight_grad,
        out_bias_grad,
        norm1_gain_grad,
        norm1_bias_grad,
        up_weight_grad,
        up_bias_grad,
        down_weight_grad,
        down_bias_grad,
        norm2_gain_grad,
        norm2_bias_grad,
    )


def solution(mesh):
    placed = (
        P(("dp", "col"), "row"),
        P(("dp", "row"), None),
        P("row", None, "col"),
        P(None, "col"),
        P("col", "row"),
        P(),
        P(),
        P(),
        P("row", "col"),
        P("col"),
        P("col", "row"),
        P(),
        P(),
        P(),
        P(("dp", "col"), "row"),
    )
    return jax.shard_map(
        shards,
        mesh=mesh,
        in_specs=placed,
        out_specs=(
            P(("dp", "col"), "row"),
            P(("dp", "col"), "row"),
            P("row", None, "col"),
            P(None, "col"),
            P("col", "row"),
            P("row"),
            P("row"),
            P("row"),
            P("row", "col"),
            P("col"),
            P("col", "row"),
            P("row"),
            P("row"),
            P("row"),
        ),
        check_vma=False,
    )
```

profile of v0, /device:TPU:0, one launch (start us, length us, event | category | flops | bytes accessed | tf_op | source)
XLA Modules:
  0.0 1307.2 jit_solution(3526439882307879938)
XLA Ops:
  9.2 49.1 %all-gather.9.cloned.1.call-done = bf16[4096,256]{1,0:T(8,128)(2,1)} async-done(((bf16[1024,256]{1,0:T(8,128)(2,1)}), bf16[4096,256]{1,0:T(8,128)(2,1)}) %all-gather.9.cloned.1.call-update) | async-done | bytes 2097168 | tf_op jit(solution)/shard_map/all_gather | solution.py:15
  58.3 8.0 fusion.72
  67.0 97.2 %reduce-scatter.9.cloned.1.call-done = f32[1024,768]{1,0:T(8,128)} async-done(((f32[4096,768]{1,0:T(8,128)}), f32[1024,768]{1,0:T(8,128)}) %reduce-scatter.9.cloned.1.call-update) | async-done | bytes 3145744 | tf_op jit(solution)/shard_map/reduce_scatter | solution.py:23
  172.2 8.6 while.22
  183.3 22.7 %all-gather.11.cloned.1.call-done = bf16[4096,256]{0,1:T(8,128)(2,1)} async-done(((bf16[1024,256]{0,1:T(8,128)(2,1)}), bf16[4096,256]{0,1:T(8,128)(2,1)}) %all-gather.11.cloned.1.call-update) | async-done | bytes 2097168 | tf_op jit(solution)/shard_map/all_gather | solution.py:19
  212.6 74.6 %reduce-scatter.11.cloned.1.call-done = f32[1024,256]{1,0:T(8,128)} async-done(((f32[4096,256]{1,0:T(8,128)}), f32[1024,256]{1,0:T(8,128)}) %reduce-scatter.11.cloned.1.call-update) | async-done | bytes 1048592 | tf_op jit(solution)/shard_map/reduce_scatter | solution.py:34
  297.4 45.4 %all-gather.13.cloned.1.call-done = bf16[4096,256]{1,0:T(8,128)(2,1)} async-done(((bf16[1024,256]{1,0:T(8,128)(2,1)}), bf16[4096,256]{1,0:T(8,128)(2,1)}) %all-gather.13.cloned.1.call-update) | async-done | bytes 2097168 | tf_op jit(solution)/shard_map/all_gather | solution.py:15
  342.8 9.7 fusion.74
  352.6 124.9 %reduce-scatter.13.cloned.1.call-done = f32[1024,1024]{1,0:T(8,128)} async-done(((f32[4096,1024]{1,0:T(8,128)}), f32[1024,1024]{1,0:T(8,128)}) %reduce-scatter.13.cloned.1.call-update) | async-done | bytes 4194320 | tf_op jit(solution)/shard_map/reduce_scatter | solution.py:23
  477.6 11.8 multiply_convert_fusion.1
  489.4 58.4 %all-gather.15.cloned.1.call-done = bf16[4096,1024]{1,0:T(8,128)(2,1)} async-done(((bf16[1024,1024]{1,0:T(8,128)(2,1)}), bf16[4096,1024]{1,0:T(8,128)(2,1)}) %all-gather.15.cloned.1.call-update) | async-done | bytes 8388624 | tf_op jit(solution)/shard_map/all_gather | solution.py:19
  557.1 75.3 %reduce-scatter.15.cloned.1.call-done = f32[1024,256]{1,0:T(8,128)} async-done(((f32[4096,256]{1,0:T(8,128)}), f32[1024,256]{1,0:T(8,128)}) %reduce-scatter.15.cloned.1.call-update) | async-done | bytes 1048592 | tf_op jit(solution)/shard_map/reduce_scatter | solution.py:34
  652.8 45.7 %all-gather.17.cloned.1.call-done = bf16[4096,256]{1,0:T(8,128)(2,1)} async-done(((bf16[1024,256]{1,0:T(8,128)(2,1)}), bf16[4096,256]{1,0:T(8,128)(2,1)}) %all-gather.17.cloned.1.call-update) | async-done | bytes 2097168 | tf_op jit(solution)/shard_map/all_gather | solution.py:15
  698.5 9.7 fusion.76
  708.7 124.5 %reduce-scatter.17.cloned.1.call-done = f32[1024,1024]{1,0:T(8,128)} async-done(((f32[4096,1024]{1,0:T(8,128)}), f32[1024,1024]{1,0:T(8,128)}) %reduce-scatter.17.cloned.1.call-update) | async-done | bytes 4194320 | tf_op jit(solution)/shard_map/reduce_scatter | solution.py:23
  839.9 58.4 %all-gather.19.cloned.1.call-done = bf16[4096,1024]{1,0:T(8,128)(2,1)} async-done(((bf16[1024,1024]{1,0:T(8,128)(2,1)}), bf16[4096,1024]{1,0:T(8,128)(2,1)}) %all-gather.19.cloned.1.call-update) | async-done | bytes 8388624 | tf_op jit(solution)/shard_map/all_gather | solution.py:19
  906.9 76.1 %reduce-scatter.19.cloned.1.call-done = f32[1024,256]{1,0:T(8,128)} async-done(((f32[4096,256]{1,0:T(8,128)}), f32[1024,256]{1,0:T(8,128)}) %reduce-scatter.19.cloned.1.call-update) | async-done | bytes 1048592 | tf_op jit(solution)/shard_map/reduce_scatter | solution.py:34
  996.2 45.6 %all-gather.21.cloned.1.call-done = bf16[4096,256]{1,0:T(8,128)(2,1)} async-done(((bf16[1024,256]{1,0:T(8,128)(2,1)}), bf16[4096,256]{1,0:T(8,128)(2,1)}) %all-gather.21.cloned.1.call-update) | async-done | bytes 2097168 | tf_op jit(solution)/shard_map/all_gather | solution.py:15
  1046.2 43.3 %reduce-scatter.21.cloned.1.call-done = f32[1024,256]{1,0:T(8,128)} async-done(((f32[4096,256]{1,0:T(8,128)}), f32[1024,256]{1,0:T(8,128)}) %reduce-scatter.21.cloned.1.call-update) | async-done | bytes 1048592 | tf_op jit(solution)/shard_map/reduce_scatter | solution.py:23
  1093.8 15.5 %while.23 = (s32[]{:T(128)}, bf16[2,512,3,4,64]{1,4,3,2,0:T(8,128)(2,1)}, bf16[2,512,4,64]{1,3,2,0:T(8,128)(2,1)S(1)}, s32[2,512]{1,0:T(2,128)S(1)}, bf16[2,512,...) while((s32[]{:T(128)}, ...), condition=%wide.region_29.30_spmd, body=%wide.region_27.29_spmd.sunk | while | flops 689960960 | bytes 49348788 | solution.py:202
  1121.5 8.0 convolution_convert_fusion.1
  1130.9 29.6 %all-gather.23.cloned.1.call-done = bf16[4096,768]{0,1:T(8,128)(2,1)} async-done(((bf16[1024,768]{0,1:T(8,128)(2,1)}), bf16[4096,768]{0,1:T(8,128)(2,1)}) %all-gather.23.cloned.1.call-update) | async-done | bytes 6291472 | tf_op jit(solution)/shard_map/all_gather | solution.py:19
  1180.1 22.1 %all-reduce = (f32[256]{0:T(256)}, f32[256]{0:T(256)}, f32[256]{0:T(256)}, f32[256]{0:T(256)}) all-reduce(f32[256]{0:T(256)S(1)} %get-tuple-element.120, f32[256]{0:T(256)S(1)} %get-tuple-element.125, f32[256]{0:T(256)S(1)} %get-tuple-element.122, f32[256]{0:T(256)S(1)} %get-tuple-element.131), channel_id=1, replica_groups=mesh['dp'=2,'row'=4,'col'=4] {'dp','col'}, use_global_device_ids=true, to_apply=%region_38.39 | all-reduce | flops 1024 | bytes 8192 | tf_op jit(solution)/shard_map/psum | solution.py:279
  1226.9 71.3 %reduce-scatter.23.cloned.1.call-done = f32[1024,256]{1,0:T(8,128)} async-done(((f32[4096,256]{1,0:T(8,128)}), f32[1024,256]{1,0:T(8,128)}) %reduce-scatter.23.cloned.1.call-update) | async-done | bytes 1048592 | tf_op jit(solution)/shard_map/reduce_scatter | solution.py:34
  (182 shorter events, 181.2 us)
Async XLA Ops:
  7.2 540.7 %copy-start = (bf16[1024,256]{1,0:T(8,128)(2,1)S(1)}, bf16[1024,256]{1,0:T(8,128)(2,1)}, u32[]{:S(2)}) copy-start(bf16[1024,256]{1,0:T(8,128)(2,1)} %param.29) | copy-start | bytes 1572868
  7.2 51.1 %all-gather.9.cloned.1.call-start = ((), (), s32[]{:S(2)}) async-start(), calls=%async_computation.8 | async-start | bytes 2621440 | tf_op jit(solution)/shard_map/all_gather | solution.py:15
  7.9 156.3 %reduce-scatter.9.cloned.1.call-start = ((), (), s32[]{:S(2)}) async-start(), calls=%async_computation.9 | async-start | bytes 15728640 | tf_op jit(solution)/shard_map/reduce_scatter | solution.py:23
  9.1 57.1 %copy-start.9 = (bf16[256,3,256]{0,2,1:T(8,128)(2,1)}, bf16[256,3,256]{0,2,1:T(8,128)(2,1)S(1)}, u32[]{:S(2)}) copy-start(bf16[256,3,256]{0,2,1:T(8,128)(2,1)S(1)} %copy.42) | copy-start | bytes 1179652
  66.3 139.7 %all-gather.11.cloned.1.call-start = ((), (), s32[]{:S(2)}) async-start(), calls=%async_computation.10 | async-start | bytes 2621440 | tf_op jit(solution)/shard_map/all_gather | solution.py:19
  183.2 104.0 %reduce-scatter.11.cloned.1.call-start = ((), (), s32[]{:S(2)}) async-start(), calls=%async_computation.11 | async-start | bytes 5242880 | tf_op jit(solution)/shard_map/reduce_scatter | solution.py:34
  210.3 132.5 %all-gather.13.cloned.1.call-start = ((), (), s32[]{:S(2)}) async-start(), calls=%async_computation.12 | async-start | bytes 2621440 | tf_op jit(solution)/shard_map/all_gather | solution.py:15
  297.2 180.4 %reduce-scatter.13.cloned.1.call-start = ((), (), s32[]{:S(2)}) async-start(), calls=%async_computation.13 | async-start | bytes 20971520 | tf_op jit(solution)/shard_map/reduce_scatter | solution.py:23
  352.5 125.0 %copy-start.16 = (f32[1024]{0:T(1024)S(1)}, f32[1024]{0:T(1024)}, u32[]{:S(2)}) copy-start(f32[1024]{0:T(1024)} %param.28) | copy-start | bytes 12292
  352.6 195.3 %all-gather.15.cloned.1.call-start = ((), (), s32[]{:S(2)}) async-start(), calls=%async_computation.14 | async-start | bytes 10485760 | tf_op jit(solution)/shard_map/all_gather | solution.py:19
  489.4 143.1 %reduce-scatter.15.cloned.1.call-start = ((), (), s32[]{:S(2)}) async-start(), calls=%async_computation.15 | async-start | bytes 5242880 | tf_op jit(solution)/shard_map/reduce_scatter | solution.py:34
  555.5 143.0 %all-gather.17.cloned.1.call-start = ((), (), s32[]{:S(2)}) async-start(), calls=%async_computation.16 | async-start | bytes 2621440 | tf_op jit(solution)/shard_map/all_gather | solution.py:15
  652.7 180.4 %reduce-scatter.17.cloned.1.call-start = ((), (), s32[]{:S(2)}) async-start(), calls=%async_computation.17 | async-start | bytes 20971520 | tf_op jit(solution)/shard_map/reduce_scatter | solution.py:23
  708.2 190.1 %all-gather.19.cloned.1.call-start = ((), (), s32[]{:S(2)}) async-start(), calls=%async_computation.18 | async-start | bytes 10485760 | tf_op jit(solution)/shard_map/all_gather | solution.py:19
  833.2 65.1 %copy-start.12 = (bf16[256,1024]{1,0:T(8,128)(2,1)S(1)}, bf16[256,1024]{1,0:T(8,128)(2,1)}, u32[]{:S(2)}) copy-start(bf16[256,1024]{1,0:T(8,128)(2,1)} %param.27) | copy-start | bytes 1572868
  839.9 143.2 %reduce-scatter.19.cloned.1.call-start = ((), (), s32[]{:S(2)}) async-start(), calls=%async_computation.19 | async-start | bytes 5242880 | tf_op jit(solution)/shard_map/reduce_scatter | solution.py:34
  906.1 77.0 %copy-start.4 = (bf16[1024,256]{1,0:T(8,128)(2,1)S(1)}, bf16[1024,256]{1,0:T(8,128)(2,1)}, u32[]{:S(2)}) copy-start(bf16[1024,256]{1,0:T(8,128)(2,1)} %param.33) | copy-start | bytes 1572868
  906.1 135.8 %all-gather.21.cloned.1.call-start = ((), (), s32[]{:S(2)}) async-start(), calls=%async_computation.20 | async-start | bytes 2621440 | tf_op jit(solution)/shard_map/all_gather | solution.py:15
  996.2 93.4 %reduce-scatter.21.cloned.1.call-start = ((), (), s32[]{:S(2)}) async-start(), calls=%async_computation.21 | async-start | bytes 5242880 | tf_op jit(solution)/shard_map/reduce_scatter | solution.py:23
  1046.2 114.4 %all-gather.23.cloned.1.call-start = ((), (), s32[]{:S(2)}) async-start(), calls=%async_computation.22 | async-start | bytes 7864320 | tf_op jit(solution)/shard_map/all_gather | solution.py:19
  1114.0 105.1 %all-reduce.9.cloned.1.call-start = ((), (), s32[]{:S(2)}) async-start(), calls=%async_computation.24 | async-start | bytes 3145728 | tf_op jit(solution)/shard_map/psum | solution.py:292
  1166.7 131.5 %reduce-scatter.23.cloned.1.call-start = ((), (), s32[]{:S(2)}) async-start(), calls=%async_computation.23 | async-start | bytes 5242880 | tf_op jit(solution)/shard_map/reduce_scatter | solution.py:34
  1204.4 93.8 %copy-start.6 = (f32[1024,256]{1,0:T(8,128)S(1)}, f32[1024,256]{1,0:T(8,128)}, u32[]{:S(2)}) copy-start(f32[1024,256]{1,0:T(8,128)} %get-tuple-element.183) | copy-start | bytes 3145732
  1204.4 96.1 %copy-start.1 = (bf16[1024,256]{1,0:T(8,128)(2,1)S(1)}, bf16[1024,256]{1,0:T(8,128)(2,1)}, u32[]{:S(2)}) copy-start(bf16[1024,256]{1,0:T(8,128)(2,1)} %param.29) | copy-start | bytes 1572868
  (15 other events, 108.4 us)
Sparse Core Ops, SparseCore 0:
  9.6 48.6 all-gather.8
  66.4 97.7 reduce-scatter.8
  183.4 22.5 all-gather.10
  210.4 76.7 reduce-scatter.10
  297.3 45.4 all-gather.12
  352.7 124.8 reduce-scatter.12
  489.5 58.2 all-gather.14
  555.6 76.7 reduce-scatter.14
  652.9 45.5 all-gather.16
  708.3 124.8 reduce-scatter.16
  840.0 58.2 all-gather.18
  906.2 76.7 reduce-scatter.18
  996.3 45.4 all-gather.20
  1046.3 43.1 reduce-scatter.20
  1114.1 46.3 all-gather.22
  1166.8 52.2 all-reduce.8
  1221.4 76.7 reduce-scatter.22
where the time goes:
time: 1320 us; the launch traced here: 1310 us
  waiting for transfers between devices  1050 us (80%)
  matrix products  94.1 us (7%)
  other arithmetic  68.7 us (5%)
  blocking collectives  54.1 us (4%)
  local copies, waits for them, and re-layouts  27.5 us (2%)
  between operations  14.5 us (1%)
    reduce_scatter x4, waiting for transfers between devices, row_product(): lax.psum_scatter(lax.dot_general(gathered, weight, (((1,), (contract,)),...  390 us
    reduce_scatter x4, waiting for transfers between devices, col_product(): lax.psum_scatter(lax.dot_general(gathered, weight, (((1,), (contract,)),...  297 us
    all_gather x4, waiting for transfers between devices, col_gather(): return lax.all_gather(values, 'col', axis=0, tiled=True)  186 us
    all_gather x4, waiting for transfers between devices, row_gather(): return lax.all_gather(values, 'row', axis=0, tiled=True)  169 us
    dot_general x4, matrix products, row_product(): lax.dot_general(gathered, weight, (((1,), (contract,)), ((), ())), prefer...  31.7 us
    psum x4, blocking collectives, row_stats(): return lax.psum((first_part, second_part), 'row')  27 us
  transfers between devices with their start and end apart: 17, of which 17 were waited for; matrix products, arithmetic and copies ran while one was open for 4% of the time, Pallas kernels for 0%

commit v1 on v0

v1 whole, which is shorter than its diff:
```python
import functools

import jax
import jax.numpy as jnp
from jax import lax
from jax.experimental import pallas as pl
from jax.experimental.pallas import tpu as pltpu
from jax.sharding import PartitionSpec as P

D = 1024
HEAD = 64
SEQ = 512
EPS = 1e-05
MESH = pl.DeviceIdType.MESH
BF = jnp.bfloat16
F32 = jnp.float32
ROWS = 128


def dot(left, right, left_dim, right_dim):
    return lax.dot_general(
        left, right, (((left_dim,), (right_dim,)), ((), ())), preferred_element_type=F32
    )


def al(index, step):
    return pl.multiple_of(index * step, step)


def col_sum(values):
    return jnp.sum(values, 0, keepdims=True)


def layer_kernel(
    seg_in,
    x_in,
    og_in,
    wq_in,
    wo_in,
    wu_in,
    wd_in,
    bias_in,
    vecs,
    lo_out,
    tg_out,
    fin_q,
    fin_o,
    fin_u,
    fin_d,
    vec_out,
    seg,
    biases,
    xf,
    wq,
    wo,
    wu,
    wd,
    proj,
    probs,
    ctx,
    mask,
    part,
    rsc,
    rsy,
    ysend,
    normed1,
    inv1,
    hf,
    act,
    gelup,
    og,
    lo,
    gsec,
    gdf,
    gu,
    gaf,
    gctx,
    gproj,
    partf,
    rscf,
    rsyf,
    ysendf,
    tg,
    gq,
    go,
    gup,
    gd,
    xq,
    xo,
    xu,
    xd,
    zq,
    zo,
    zu,
    zd,
    ss,
    rs,
    ls,
):
    d = lax.axis_index("dp")
    r = lax.axis_index("row")
    c = lax.axis_index("col")
    y = r // 2
    k = r % 2
    p = d % 2
    r1 = r + 1 - 2 * k
    r2 = (r + 2) % 4
    r3 = (r1 + 2) % 4
    kc = c // 2
    ic = c % 2
    is_agg = k == kc
    core_dev = (d, r1, c)
    y_dev = (d, r2, c)
    x_dev = (d + 1 - 2 * p, r, c)

    counts = {"s": 0, "r": 0, "l": 0}

    def new(kind, n=1):
        at = counts[kind]
        counts[kind] += n
        return at

    def remote(si, ri, src, dst, dev):
        return pltpu.make_async_remote_copy(
            src_ref=src,
            dst_ref=dst,
            send_sem=ss.at[si],
            recv_sem=rs.at[ri],
            device_id=dev,
            device_id_type=MESH,
        )

    late = []

    def later(copy, condition=None):
        late.append((condition, copy))

    barrier = pltpu.get_barrier_semaphore()
    for j in (1, 2, 3):
        pl.semaphore_signal(barrier, inc=1, device_id=(d, (r + j) % 4, c), device_id_type=MESH)
        pl.semaphore_signal(barrier, inc=1, device_id=(d, r, (c + j) % 4), device_id_type=MESH)
    pl.semaphore_signal(barrier, inc=1, device_id=x_dev, device_id_type=MESH)

    @pl.when(r != c)
    def _():
        pl.semaphore_signal(barrier, inc=1, device_id=(d, c, r), device_id_type=MESH)
        pl.semaphore_wait(barrier, 8)

    @pl.when(r == c)
    def _():
        pl.semaphore_wait(barrier, 7)

    def qkv_piece(yp):
        return wq_in.at[:, :, pl.ds(al(yp, 384), 384)]

    def out_piece(yp):
        return wo_in.at[yp]

    def up_piece(yp):
        return wu_in.at[:, :, pl.ds(al(yp, 512), 512)]

    def down_piece(yp):
        return wd_in.at[yp]

    def qkv_place(row):
        return wq.at[row, :, :, pl.ds(al(ic, 384), 384)]

    def out_place(row):
        return wo.at[ic, :, :, pl.ds(al(row, 256), 256)]

    def up_place(row):
        return wu.at[row, :, :, pl.ds(al(ic, 512), 512)]

    def down_place(row):
        return wd.at[ic, :, :, pl.ds(al(row, 256), 256)]

    def qkv_half(ref, half, ci):
        return ref.at[:, half, :, pl.ds(al(ci, 384), 384)]

    def out_half(ref, half, ci):
        return ref.at[ci, half]

    def up_half(ref, half, ci):
        return ref.at[:, half, :, pl.ds(al(ci, 512), 512)]

    def down_half(ref, half, ci):
        return ref.at[ci, half]

    class Weight:
        def __init__(self, buffer, piece, place, half):
            self.buffer, self.piece, self.place, self.half = buffer, piece, place, half
            self.s1, self.r1, self.l1 = new("s", 2), new("r", 4), new("l")
            self.s2, self.r2 = new("s", 3), new("r", 4)
            self.s3, self.r3 = new("s", 2), new("r", 2)

        def spread_rows(self):
            other = remote(
                self.s1, self.r1 + r, self.piece(1 - y), self.place(r), (d, 2 * (1 - y) + kc, c)
            )
            other.start()
            later(other)
            near = remote(self.s1 + 1, self.r1 + r, self.piece(y), self.place(r), core_dev)
            own = pltpu.make_async_copy(self.piece(y), self.place(r), ls.at[self.l1])

            @pl.when(jnp.logical_not(is_agg))
            def _():
                near.start()

            later(near, jnp.logical_not(is_agg))

            @pl.when(is_agg)
            def _():
                own.start()

            self.own = own

        def spread_cols(self):
            copies = []
            for j in (1, 2, 3):
                region = self.half(self.buffer, p, ic)
                copies.append(
                    remote(self.s2 + j - 1, self.r2 + c, region, region, (d, r, (c + j) % 4))
                )

            @pl.when(is_agg)
            def _():
                self.own.wait()
                for j in (1, 2, 3):
                    row = (r + j) % 4
                    remote(
                        self.s1, self.r1 + row, self.place(row), self.place(row), core_dev
                    ).wait_recv()
                for copy in copies:
                    copy.start()

            for copy in copies:
                later(copy, is_agg)

        def spread_pair(self):
            for ci in (0, 1):
                source = 2 * k + ci
                region = self.half(self.buffer, p, ci)
                copy = remote(self.s3 + ci, self.r3 + ci, region, region, x_dev)

                @pl.when(source != c)
                def _():
                    remote(self.s2, self.r2 + source, region, region, x_dev).wait_recv()
                    copy.start()

                later(copy, source != c)

        def ready(self):
            for ci in (0, 1):
                region = self.half(self.buffer, 1 - p, ci)

                @pl.when(2 * k + ci != c)
                def _():
                    remote(self.s3 + ci, self.r3 + ci, region, region, x_dev).wait_recv()

    w_qkv = Weight(wq, qkv_piece, qkv_place, qkv_half)
    w_out = Weight(wo, out_piece, out_place, out_half)
    w_up = Weight(wu, up_piece, up_place, up_half)
    w_down = Weight(wd, down_piece, down_place, down_half)

    def rows_of(ref, s, row):
        return ref.at[s, pl.ds(al(row, ROWS), ROWS), :]

    def slab_of(ref, s, row):
        return ref.at[s, :, pl.ds(al(row, 256), 256)]

    class Gather:
        def __init__(self, full, at, s, source=None):
            self.full, self.at, self.s = full, at, s
            self.source = source
            self.si, self.ri = new("s", 3), new("r", 3)

        def send(self):
            mine = self.source if self.source is not None else self.at(self.full, self.s, r)
            place = self.at(self.full, self.s, r)
            for n, dev in ((0, y_dev), (1, core_dev)):
                copy = remote(self.si + n, self.ri + n, mine, place, dev)
                copy.start()
                later(copy)

        def forward(self):
            place = self.at(self.full, self.s, r2)
            remote(self.si, self.ri, place, place, y_dev).wait_recv()
            copy = remote(self.si + 2, self.ri + 2, place, place, core_dev)
            copy.start()
            later(copy)

        def wait(self):
            near = self.at(self.full, self.s, r1)
            remote(self.si, self.ri + 1, near, near, core_dev).wait_recv()
            far = self.at(self.full, self.s, r3)
            remote(self.si, self.ri + 2, far, far, core_dev).wait_recv()

    class Scatter:
        def __init__(self, source, at, core_recv, y_send, y_recv, s):
            self.source, self.at = source, at
            self.core_recv, self.y_send, self.y_recv, self.s = core_recv, y_send, y_recv, s
            si, ri = new("s", 3), new("r", 3)
            self.far = remote(si, ri, at(source, s, r3), core_recv.at[s, 1], core_dev)
            self.near = remote(si + 1, ri + 1, at(source, s, r1), core_recv.at[s, 0], core_dev)
            self.cross = remote(si + 2, ri + 2, y_send.at[s], y_recv.at[s], y_dev)

        def to_core(self):
            self.far.start()
            self.near.start()

        def to_y(self):
            self.far.wait_recv()
            total = self.at(self.source, self.s, r2)[...].astype(F32)
            self.y_send[self.s] = (total + self.core_recv[self.s, 1].astype(F32)).astype(BF)
            self.cross.start()

        def result(self):
            self.near.wait_recv()
            total = self.at(self.source, self.s, r)[...].astype(F32)
            total = total + self.core_recv[self.s, 0].astype(F32)
            self.cross.wait_recv()
            return total + self.y_recv[self.s].astype(F32)

        def sent(self):
            self.far.wait_send()
            self.near.wait_send()
            self.cross.wait_send()

    w_qkv.spread_rows()
    x_gather = [Gather(xf, slab_of, s, x_in.at[s]) for s in (0, 1)]
    x_own = [
        pltpu.make_async_copy(x_in.at[s], slab_of(xf, s, r), ls.at[new("l")]) for s in (0, 1)
    ]
    seg_s, seg_r, seg_l = new("s"), new("r"), new("l")
    seg_copy = remote(seg_s, seg_r, seg_in, seg, (d, c, r))
    seg_own = pltpu.make_async_copy(seg_in, seg, ls.at[seg_l])

    @pl.when(r != c)
    def _():
        seg_copy.start()

    @pl.when(r == c)
    def _():
        seg_own.start()

    bias_s, bias_r = new("s", 3), new("r", 4)
    for j in (1, 2, 3):
        copy = remote(
            bias_s + j - 1, bias_r + c, bias_in, biases.at[c], (d, r, (c + j) % 4)
        )
        copy.start()
        later(copy)
    biases[c] = bias_in[...]
    for s in (0, 1):
        x_gather[s].send()
        x_own[s].start()

    w_qkv.spread_cols()
    w_out.spread_rows()
    w_up.spread_rows()
    x_gather[0].forward()
    w_qkv.spread_pair()
    x_gather[1].forward()
    w_out.spread_cols()
    w_up.spread_cols()
    w_down.spread_rows()

    og_s, og_r, og_l = new("s", 3), new("r", 4), new("l")

    def og_place(row):
        return og.at[:, :, pl.ds(al(row, 256), 256)]

    og_own = pltpu.make_async_copy(og_in.at[:, pl.ds(al(r, ROWS), ROWS), :], og_place(r), ls.at[og_l])
    og_own.start()
    for j in (1, 2, 3):
        row = (r + j) % 4
        copy = remote(
            og_s + j - 1,
            og_r + r,
            og_in.at[:, pl.ds(al(row, ROWS), ROWS), :],
            og_place(r),
            (d, row, c),
        )
        copy.start()
        later(copy)

    for j in (1, 2, 3):
        source = (c + j) % 4
        remote(bias_s, bias_r + source, biases.at[source], biases.at[source], core_dev).wait_recv()

    @pl.when(r != c)
    def _():
        seg_copy.wait_recv()

    @pl.when(r == c)
    def _():
        seg_own.wait()

    later(seg_copy, r != c)
    w_qkv.ready()

    vec_out[...] = jnp.zeros_like(vec_out)

    def project(s):
        rows = xf[s]

        def half(ci, carry):
            weight = wq[:, :, :, pl.ds(al(ci, 384), 384)].reshape(D, 384)
            q_bias = biases[2 * k + ci, 1:2, pl.ds(al(y, 128), 128)]
            v_bias = biases[2 * k + ci, 1:2, pl.ds(pl.multiple_of(256 + y * 128, 128), 128)]
            bias = jnp.concatenate([q_bias, jnp.zeros_like(q_bias), v_bias], 1)
            proj[s, :, pl.ds(al(ci, 384), 384)] = (dot(rows, weight, 1, 0) + bias).astype(BF)
            return carry

        lax.fori_loop(0, 2, half, 0)

    def columns(ci, n):
        return pl.ds(pl.multiple_of(ci * 384 + n * 128, 128), 128)

    def attend(s):
        labels = seg[s : s + 1, :]
        down = jnp.transpose(jnp.broadcast_to(labels, (128, SEQ)))[:, 0:1]
        mask[...] = jnp.where(down == labels, 0.0, -1e30)
        lane = lax.broadcasted_iota(jnp.int32, (SEQ, 128), 1)
        row = lax.broadcasted_iota(jnp.int32, (128, SEQ), 0)

        def pair(ci, carry):
            queries = proj[s, :, columns(ci, 0)]
            keys_in = proj[s, :, columns(ci, 1)]
            values_in = proj[s, :, columns(ci, 2)]
            parts = []
            for h in (0, 1):
                chosen = (lane < HEAD) if h == 0 else (lane >= HEAD)
                masked = jnp.where(chosen, queries, jnp.zeros_like(queries))
                scores = dot(keys_in, masked, 1, 1) * (float(HEAD) ** (-0.5)) + mask[...]
                weights = jnp.exp(scores - jnp.max(scores, 0, keepdims=True))
                totals = jnp.sum(weights, 0, keepdims=True)
                share = (weights * (1.0 / totals)).astype(BF)
                probs[s, ci * 2 + h] = share
                parts.append(dot(values_in, share, 0, 0))
            both = jnp.where(row < HEAD, parts[0], parts[1])
            ctx[s, :, pl.ds(al(ci, 128), 128)] = jnp.transpose(both).astype(BF)
            return carry

        lax.fori_loop(0, 2, pair, 0)

    def out_partial(s):
        part[s] = dot(ctx[s], wo[...].reshape(256, D), 1, 0).astype(BF)

    def norm_stats(summed):
        center = jnp.sum(summed, 1, keepdims=True) * (1.0 / D)
        spread = jnp.sum(summed * summed, 1, keepdims=True) * (1.0 / D) - center * center
        inverse = lax.rsqrt(spread + EPS)
        return (summed - center) * inverse, inverse

    def norm_pull(grad, normed, inverse, gain):
        scaled = grad * gain
        first = jnp.sum(scaled, 1, keepdims=True) * (1.0 / D)
        second = jnp.sum(scaled * normed, 1, keepdims=True) * (1.0 / D)
        return inverse * (scaled - first - normed * second)

    out_bias, gain1, offset1 = vecs[0:1, :], vecs[1:2, :], vecs[2:3, :]
    down_bias, gain2, offset2 = vecs[3:4, :], vecs[4:5, :], vecs[5:6, :]
    own_rows = pl.ds(al(r, ROWS), ROWS)

    def scatters():
        return [Scatter(part, rows_of, rsc, ysend, rsy, s) for s in (0, 1)]

    rs1 = scatters()
    ag1 = [Gather(hf, rows_of, s) for s in (0, 1)]

    def first_norm(s):
        first_sum = rs1[s].result() + out_bias + xf[s, own_rows, :].astype(F32)
        normed, inverse = norm_stats(first_sum)
        normed1[s] = normed
        inv1[s] = jnp.broadcast_to(inverse, (ROWS, 128))
        hf[s, own_rows, :] = (normed * gain1 + offset1).astype(BF)
        ag1[s].send()

    for s in (0, 1):
        if s == 0:
            x_own[0].wait()
            x_gather[0].wait()
        else:
            x_own[1].wait()
            x_gather[1].wait()
        project(s)
        if s == 0:
            w_out.spread_pair()
            w_down.spread_cols()
        attend(s)
        if s == 0:
            w_out.ready()
        else:
            w_up.spread_pair()
        out_partial(s)
        rs1[s].to_core()
        rs1[s].to_y()
    first_norm(0)
    ag1[0].forward()
    first_norm(1)
    w_down.spread_pair()
    w_up.ready()
    ag1[0].wait()

    def up_bias_of(ci):
        return biases[2 * k + ci, 0:1, pl.ds(al(y, 512), 512)]

    def mlp_up(s):
        rows = hf[s]

        def tile(n, carry):
            cols = pl.ds(al(n, 256), 256)
            weight = wu[:, :, :, cols].reshape(D, 256)
            ci = n // 2
            bias = biases[2 * k + ci, 0:1, pl.ds(pl.multiple_of(y * 512 + (n % 2) * 256, 256), 256)]
            upward = dot(rows, weight, 1, 0) + bias
            share = 0.5 + 0.5 * lax.erf(upward * 0.7071067811865476)
            act[s, :, cols] = (upward * share).astype(BF)
            density = jnp.exp(-0.5 * upward * upward) * 0.3989422804014327
            gelup[s, :, cols] = (share + upward * density).astype(BF)
            return carry

        lax.fori_loop(0, 4, tile, 0)

    def mlp_down(s):
        rows = act[s]

        def tile(n, carry):
            cols = pl.ds(al(n, 256), 256)
            weight = wd[:, :, :, cols].reshape(D, 256)
            part[s, :, cols] = dot(rows, weight, 1, 0).astype(BF)
            return carry

        lax.fori_loop(0, 4, tile, 0)

    rs2 = scatters()
    ag2 = [Gather(gdf, rows_of, s) for s in (0, 1)]
    lo_s, lo_r, lo_l = new("s", 6), new("r", 8), new("l", 2)

    og_own.wait()
    for j in (1, 2, 3):
        source = (r + j) % 4
        remote(og_s, og_r + source, og_place(source), og_place(source), core_dev).wait_recv()

    def second_norm(s):
        hidden = normed1[s] * gain1 + offset1
        second_sum = rs2[s].result() + down_bias + hidden
        normed, inverse = norm_stats(second_sum)
        lo[s] = (normed * gain2 + offset2).astype(BF)
        grad = og[s].astype(F32)
        vec_out[0:1, :] += col_sum(grad * normed)
        vec_out[1:2, :] += col_sum(grad)
        grad_second = norm_pull(grad, normed, inverse, gain2)
        gsec[s] = grad_second
        rounded = grad_second.astype(BF)
        vec_out[4:5, :] += col_sum(rounded.astype(F32))
        gdf[s, own_rows, :] = rounded
        ag2[s].send()

    def lo_place(s, row):
        return lo_out.at[s, pl.ds(al(row, ROWS), ROWS), :]

    def lo_part(s, row):
        return lo.at[s, :, pl.ds(al(row, 256), 256)]

    lo_own = [
        pltpu.make_async_copy(lo_part(s, r), lo_place(s, r), ls.at[lo_l + s]) for s in (0, 1)
    ]

    def send_lo(s):
        lo_own[s].start()
        for j in (1, 2, 3):
            row = (r + j) % 4
            copy = remote(
                lo_s + 3 * s + j - 1, lo_r + 4 * s + r, lo_part(s, row), lo_place(s, r), (d, row, c)
            )
            copy.start()
            later(copy)

    for s in (0, 1):
        if s == 1:
            ag1[1].wait()
        mlp_up(s)
        if s == 0:
            ag1[1].forward()
            w_down.ready()
        rs1[s].sent()
        mlp_down(s)
        rs2[s].to_core()
        rs2[s].to_y()
    second_norm(0)
    ag2[0].forward()
    second_norm(1)
    ag2[0].wait()

    def pull_act(s):
        rows = gdf[s]

        def tile(n, carry):
            cols = pl.ds(al(n, 256), 256)
            grad = dot(rows, wd[n // 2, n % 2], 1, 1) * gelup[s, :, cols].astype(F32)
            rounded = grad.astype(BF)
            gu[s, :, cols] = rounded
            vec_out[6:7, cols] += col_sum(rounded.astype(F32))
            return carry

        lax.fori_loop(0, 4, tile, 0)

    def pull_hidden(s):
        rows = gu[s]

        def tile(n, carry):
            weight = wu[n].reshape(256, D)
            part[s, :, pl.ds(al(n, 256), 256)] = dot(rows, weight, 1, 1).astype(BF)
            return carry

        lax.fori_loop(0, 4, tile, 0)

    rs3 = scatters()
    ag3 = [Gather(gaf, rows_of, s) for s in (0, 1)]

    def first_norm_pull(s):
        grad = gsec[s] + rs3[s].result()
        normed = normed1[s]
        vec_out[2:3, :] += col_sum(grad * normed)
        vec_out[3:4, :] += col_sum(grad)
        rounded = norm_pull(grad, normed, inv1[s][:, 0:1], gain1).astype(BF)
        vec_out[5:6, :] += col_sum(rounded.astype(F32))
        gaf[s, own_rows, :] = rounded
        ag3[s].send()

    for s in (0, 1):
        if s == 1:
            ag2[1].wait()
        pull_act(s)
        if s == 0:
            ag2[1].forward()
        rs2[s].sent()
        pull_hidden(s)
        rs3[s].to_core()
        rs3[s].to_y()
        send_lo(s)

    class Grad:
        def __init__(self, buffer, half, pair_half, pair_recv, col_recv, piece, place, fin_half):
            self.buffer, self.half, self.pair_half = buffer, half, pair_half
            self.pair_recv, self.col_recv = pair_recv, col_recv
            self.piece, self.place, self.fin_half = piece, place, fin_half
            self.s1, self.r1 = new("s"), new("r")
            self.s2, self.r2 = new("s", 2), new("r", 3)
            self.s3, self.r3, self.l3 = new("s", 3), new("r", 2), new("l")
            self.s4, self.r4 = new("s"), new("r")
            self.pair = remote(
                self.s1, self.r1, self.pair_half(self.buffer, 1 - p), self.pair_recv, x_dev
            )

        def to_pair(self):
            self.pair.start()
            later(self.pair)

        def to_cols(self):
            self.pair.wait_recv()
            mine = self.pair_half(self.buffer, p)
            mine[...] = (mine[...].astype(F32) + self.pair_recv[...].astype(F32)).astype(BF)
            for ci in (0, 1):
                owner = 2 * k + ci
                slot = (c - owner + 3) % 4
                copy = remote(
                    self.s2 + ci,
                    self.r2 + slot,
                    self.half(self.buffer, p, ci),
                    self.col_recv.at[slot],
                    (d, r, owner),
                )

                @pl.when(owner != c)
                def _():
                    copy.start()

                later(copy, owner != c)

        def to_rows(self):
            own = pltpu.make_async_copy(self.piece(r), self.place(y), ls.at[self.l3])
            self.own = own
            copies = []
            for j in (1, 2, 3):
                row = (r + j) % 4
                copies.append(
                    remote(self.s3 + j - 1, self.r3 + y, self.piece(row), self.place(y), (d, row, c))
                )

            @pl.when(is_agg)
            def _():
                for slot in (0, 1, 2):
                    dst = self.col_recv.at[slot]
                    remote(self.s2, self.r2 + slot, dst, dst, core_dev).wait_recv()
                mine = self.half(self.buffer, p, ic)
                total = mine[...].astype(F32)
                for slot in (0, 1, 2):
                    total = total + self.col_recv[slot].astype(F32)
                mine[...] = total.astype(BF)
                own.start()
                for copy in copies:
                    copy.start()

            for copy in copies:
                later(copy, is_agg)

        def to_pair_again(self):
            @pl.when(is_agg)
            def _():
                self.own.wait()
                place = self.place(1 - y)
                remote(self.s3, self.r3 + 1 - y, place, place, core_dev).wait_recv()

            @pl.when(jnp.logical_not(is_agg))
            def _():
                for yp in (0, 1):
                    place = self.place(yp)
                    remote(self.s3, self.r3 + yp, place, place, core_dev).wait_recv()

            self.last = remote(self.s4, self.r4, self.fin_half(p), self.fin_half(p), x_dev)
            self.last.start()
            later(self.last)

        def done(self):
            dst = self.fin_half(1 - p)
            remote(self.s4, self.r4, dst, dst, x_dev).wait_recv()

    def lead_half(ref, half):
        return ref.at[:, half]

    g_qkv = Grad(
        gq,
        qkv_half,
        lead_half,
        xq,
        zq,
        lambda row: gq.at[row, p, :, pl.ds(al(ic, 384), 384)],
        lambda yp: fin_q.at[p, :, pl.ds(al(yp, 384), 384)],
        lambda half: fin_q.at[half],
    )
    g_out = Grad(
        go,
        out_half,
        lead_half,
        xo,
        zo,
        lambda row: go.at[ic, p, :, pl.ds(al(row, 256), 256)],
        lambda yp: fin_o.at[yp, p],
        lambda half: fin_o.at[:, half],
    )
    g_up = Grad(
        gup,
        up_half,
        lead_half,
        xu,
        zu,
        lambda row: gup.at[row, p, :, pl.ds(al(ic, 512), 512)],
        lambda yp: fin_u.at[p, :, pl.ds(al(yp, 512), 512)],
        lambda half: fin_u.at[half],
    )
    g_down = Grad(
        gd,
        down_half,
        lead_half,
        xd,
        zd,
        lambda row: gd.at[ic, p, :, pl.ds(al(row, 256), 256)],
        lambda yp: fin_d.at[yp, p],
        lambda half: fin_d.at[:, half],
    )

    def tokens_by(ref, cols):
        return ref[:, :, cols].reshape(2 * SEQ, cols.size)

    def down_grad():
        def tile(n, carry):
            left = tokens_by(act, pl.ds(al(n, 256), 256))
            gd[n // 2, n % 2] = dot(left, gdf[...].reshape(2 * SEQ, D), 0, 0).astype(BF)
            return carry

        lax.fori_loop(0, 4, tile, 0)

    def up_grad():
        def tile(n, carry):
            left = tokens_by(hf, pl.ds(al(n, 256), 256))
            gup[n] = (
                dot(left, gu[...].reshape(2 * SEQ, D), 0, 0).astype(BF).reshape(2, 128, D)
            )
            return carry

        lax.fori_loop(0, 4, tile, 0)

    def out_grad():
        left = ctx[...].reshape(2 * SEQ, 256)
        go[...] = dot(left, gaf[...].reshape(2 * SEQ, D), 0, 0).astype(BF).reshape(2, 2, 64, D)

    def qkv_grad():
        def tile(n, carry):
            left = tokens_by(xf, pl.ds(al(n, 256), 256))
            gq[n] = (
                dot(left, gproj[...].reshape(2 * SEQ, 768), 0, 0).astype(BF).reshape(2, 128, 768)
            )
            return carry

        lax.fori_loop(0, 4, tile, 0)

    down_grad()
    g_down.to_pair()
    first_norm_pull(0)
    ag3[0].forward()
    first_norm_pull(1)
    up_grad()
    g_up.to_pair()
    ag3[0].wait()

    def pull_attend(s):
        gctx[...] = dot(gaf[s], wo[...].reshape(256, D), 1, 1).astype(BF)
        lane = lax.broadcasted_iota(jnp.int32, (SEQ, 128), 1)
        row = lax.broadcasted_iota(jnp.int32, (128, SEQ), 0)
        scale_factor = float(HEAD) ** (-0.5)

        def pair(ci, carry):
            queries = proj[s, :, columns(ci, 0)]
            keys_in = proj[s, :, columns(ci, 1)]
            values_in = proj[s, :, columns(ci, 2)]
            grad = gctx[:, pl.ds(al(ci, 128), 128)]
            grads_q, grads_k, grads_v = [], [], []
            for h in (0, 1):
                chosen = (lane < HEAD) if h == 0 else (lane >= HEAD)
                masked = jnp.where(chosen, grad, jnp.zeros_like(grad))
                share = probs[s, ci * 2 + h]
                wide = share.astype(F32)
                weighted = wide * dot(values_in, masked, 1, 1)
                total = jnp.sum(weighted, 0, keepdims=True)
                grad_scores = (weighted - wide * total).astype(BF)
                grads_v.append(dot(share, grad, 1, 0))
                grads_k.append(dot(grad_scores, queries, 1, 0))
                grads_q.append(dot(keys_in, grad_scores, 0, 0))
            both_q = jnp.transpose(jnp.where(row < HEAD, grads_q[0], grads_q[1]) * scale_factor)
            both_q = both_q.astype(BF)
            both_v = jnp.where(lane < HEAD, grads_v[0], grads_v[1]).astype(BF)
            both_k = jnp.where(lane < HEAD, grads_k[0], grads_k[1]) * scale_factor
            gproj[s, :, columns(ci, 0)] = both_q
            gproj[s, :, columns(ci, 1)] = both_k.astype(BF)
            gproj[s, :, columns(ci, 2)] = both_v
            at = pl.ds(al(ci, 128), 128)
            vec_out[7:8, at] += col_sum(both_q.astype(F32))
            at = pl.ds(pl.multiple_of(256 + ci * 128, 128), 128)
            vec_out[7:8, at] += col_sum(both_v.astype(F32))
            return carry

        lax.fori_loop(0, 2, pair, 0)

    def pull_tokens(s):
        rows = gproj[s]

        def tile(n, carry):
            partf[s, n] = dot(rows, wq[n].reshape(256, 768), 1, 1).astype(BF)
            return carry

        lax.fori_loop(0, 4, tile, 0)

    rs4 = [Scatter(partf, lambda ref, s, row: ref.at[s, row], rscf, ysendf, rsyf, s) for s in (0, 1)]
    tg_l = new("l", 2)
    tg_copy = [pltpu.make_async_copy(tg.at[s], tg_out.at[s], ls.at[tg_l + s]) for s in (0, 1)]

    def tokens_done(s):
        tg[s] = rs4[s].result() + slab_of(gaf, s, r)[...].astype(F32)
        tg_copy[s].start()

    for s in (0, 1):
        if s == 1:
            ag3[1].wait()
        pull_attend(s)
        if s == 0:
            ag3[1].forward()
            g_down.to_cols()
        else:
            g_up.to_cols()
        pull_tokens(s)
        rs4[s].to_core()
        rs4[s].to_y()
    qkv_grad()
    g_qkv.to_pair()
    out_grad()
    g_out.to_pair()
    g_down.to_rows()
    tokens_done(0)
    g_up.to_rows()
    g_qkv.to_cols()
    g_out.to_cols()
    tokens_done(1)
    g_down.to_pair_again()
    g_up.to_pair_again()
    g_qkv.to_rows()
    g_out.to_rows()
    g_qkv.to_pair_again()
    g_out.to_pair_again()
    for grad in (g_down, g_up, g_qkv, g_out):
        grad.done()

    for s in (0, 1):
        rs3[s].sent()
        rs4[s].sent()
        tg_copy[s].wait()
        lo_own[s].wait()
        for j in (1, 2, 3):
            source = (r + j) % 4
            place = lo_place(s, source)
            remote(lo_s, lo_r + 4 * s + source, place, place, core_dev).wait_recv()
    for condition, copy in late:
        if condition is None:
            copy.wait_send()
        else:
            pl.when(condition)(copy.wait_send)


S_SEMS = 160
R_SEMS = 160
L_SEMS = 32


def run_layer(seg, x, og, wq, wo, wu, wd, bias, vecs):
    any_spec = pl.BlockSpec(memory_space=pl.ANY)
    vmem = pl.BlockSpec(memory_space=pltpu.VMEM)
    out = jax.ShapeDtypeStruct
    outs = [
        (out((2, SEQ, 256), BF), any_spec),
        (out((2, SEQ, 256), F32), any_spec),
        (out((2, 128, 768), BF), any_spec),
        (out((2, 2, 64, 256), BF), any_spec),
        (out((2, 128, D), BF), any_spec),
        (out((2, 2, 256, 256), BF), any_spec),
        (out((8, D), F32), vmem),
    ]
    full = ((2, SEQ, D), BF)
    scratch = [
        ((8, SEQ), F32),
        ((4, 8, D), F32),
        full,
        ((4, 2, 128, 768), BF),
        ((2, 2, 64, D), BF),
        ((4, 2, 128, D), BF),
        ((2, 2, 256, D), BF),
        ((2, SEQ, 768), BF),
        ((2, 4, SEQ, SEQ), BF),
        ((2, SEQ, 256), BF),
        ((SEQ, SEQ), F32),
        full,
        ((2, 2, ROWS, D), BF),
        ((2, ROWS, D), BF),
        ((2, ROWS, D), BF),
        ((2, ROWS, D), F32),
        ((2, ROWS, 128), F32),
        full,
        full,
        full,
        ((2, ROWS, D), BF),
        ((2, ROWS, D), BF),
        ((2, ROWS, D), F32),
        full,
        full,
        full,
        ((SEQ, 256), BF),
        ((2, SEQ, 768), BF),
        ((2, 4, SEQ, 256), BF),
        ((2, 2, SEQ, 256), BF),
        ((2, SEQ, 256), BF),
        ((2, SEQ, 256), BF),
        ((2, SEQ, 256), F32),
        ((4, 2, 128, 768), BF),
        ((2, 2, 64, D), BF),
        ((4, 2, 128, D), BF),
        ((2, 2, 256, D), BF),
        ((4, 128, 768), BF),
        ((2, 64, D), BF),
        ((4, 128, D), BF),
        ((2, 256, D), BF),
        ((3, 4, 128, 384), BF),
        ((3, 64, D), BF),
        ((3, 4, 128, 512), BF),
        ((3, 256, D), BF),
    ]
    return pl.pallas_call(
        layer_kernel,
        out_shape=[o[0] for o in outs],
        in_specs=[any_spec] * 7 + [vmem] * 2,
        out_specs=[o[1] for o in outs],
        scratch_shapes=[pltpu.VMEM(shape, dtype) for shape, dtype in scratch]
        + [
            pltpu.SemaphoreType.DMA((S_SEMS,)),
            pltpu.SemaphoreType.DMA((R_SEMS,)),
            pltpu.SemaphoreType.DMA((L_SEMS,)),
        ],
        compiler_params=pltpu.CompilerParams(
            collective_id=0, has_side_effects=True, vmem_limit_bytes=62 * 1024 * 1024
        ),
        name="layer",
    )(seg, x, og, wq, wo, wu, wd, bias, vecs)


def shards(
    pairs,
    tokens,
    segments,
    qkv_weight,
    qv_bias,
    out_weight,
    out_bias,
    norm1_gain,
    norm1_bias,
    up_weight,
    up_bias,
    down_weight,
    down_bias,
    norm2_gain,
    norm2_bias,
    out_grad,
):
    row = lax.axis_index("row")
    col = lax.axis_index("col")
    y, k = row // 2, row % 2
    labels = jnp.pad(segments.astype(F32), ((0, 6), (0, 0)))
    wq = qkv_weight.reshape(256, 3, 2, 128).transpose(0, 2, 1, 3).reshape(2, 128, 768)
    bias = jnp.zeros((8, D), F32)
    bias = bias.at[0].set(up_bias).at[1, :512].set(qv_bias.reshape(512))
    vecs = jnp.stack(
        [out_bias, norm1_gain, norm1_bias, down_bias, norm2_gain, norm2_bias, out_bias, out_bias]
    )
    lo, tg, fin_q, fin_o, fin_u, fin_d, vec = run_layer(
        labels,
        tokens.reshape(2, SEQ, 256),
        out_grad.reshape(2, SEQ, 256),
        wq,
        out_weight.reshape(2, 2, 64, 256),
        up_weight.reshape(2, 128, D),
        down_weight.reshape(2, 2, 256, 256),
        bias,
        vecs,
    )
    up_part = lax.dynamic_update_slice(
        jnp.zeros((4, 2, 512), F32), vec[6].reshape(2, 1, 512), (2 * k, y, 0)
    )
    qv_part = lax.dynamic_update_slice(
        jnp.zeros((2, 4, 2, 128), F32), vec[7, :512].reshape(2, 2, 1, 128), (0, 2 * k, y, 0)
    )
    joined = jnp.concatenate([vec[:6].reshape(-1), up_part.reshape(-1), qv_part.reshape(-1)])
    joined = lax.psum(joined, ("dp", "row", "col"))
    features = lax.dynamic_slice_in_dim(joined[: 6 * D].reshape(6, D), row * 256, 256, 1)
    up_bias_grad = lax.dynamic_slice_in_dim(joined[6 * D : 10 * D], col * D, D)
    qv_bias_grad = lax.dynamic_slice_in_dim(joined[10 * D :].reshape(2, D), col * 256, 256, 1)
    grads = (fin_q, fin_o, fin_u, fin_d)
    if pairs is not None:
        grads = lax.psum(grads, "dp", axis_index_groups=pairs)
    fin_q, fin_o, fin_u, fin_d = grads
    fin_q = fin_q.reshape(256, 2, 3, 128).transpose(0, 2, 1, 3).reshape(256, 3, 256)
    return (
        lo.reshape(2 * SEQ, 256),
        tg.reshape(2 * SEQ, 256),
        fin_q.astype(F32),
        qv_bias_grad,
        fin_o.reshape(256, 256).astype(F32),
        features[5],
        features[2],
        features[3],
        fin_u.reshape(256, D).astype(F32),
        up_bias_grad,
        fin_d.reshape(D, 256).astype(F32),
        features[4],
        features[0],
        features[1],
    )


def solution(mesh):
    placed = (
        P(("dp", "col"), "row"),
        P(("dp", "row"), None),
        P("row", None, "col"),
        P(None, "col"),
        P("col", "row"),
        P(),
        P(),
        P(),
        P("row", "col"),
        P("col"),
        P("col", "row"),
        P(),
        P(),
        P(),
        P(("dp", "col"), "row"),
    )
    dp = mesh.shape["dp"]
    pairs = None
    if dp > 2:
        pairs = [list(range(0, dp, 2)), list(range(1, dp, 2))]
    return jax.shard_map(
        functools.partial(shards, pairs),
        mesh=mesh,
        in_specs=placed,
        out_specs=(
            P(("dp", "col"), "row"),
            P(("dp", "col"), "row"),
            P("row", None, "col"),
            P(None, "col"),
            P("col", "row"),
            P("row"),
            P("row"),
            P("row"),
            P("row", "col"),
            P("col"),
            P("col", "row"),
            P("row"),
            P("row"),
            P("row"),
        ),
        check_vma=False,
    )
```

time: 1320 us -> 304 us (0.23)
  waiting for transfers between devices: 1050 us -> 0 us
  Pallas kernels: 0 us -> 244 us
  matrix products: 94.1 us -> 0 us
  other arithmetic: 68.7 us -> 2.94 us
  local copies, waits for them, and re-layouts: 27.5 us -> 11.9 us
  between operations: 14.5 us -> 0.91 us
    reduce_scatter x8 -> x0, waiting for transfers between devices: 687 us -> none  [the longest x4 390 us: row_product(): lax.psum_scatter(lax.dot_general(gathered, weight, (((1,), (contract,)),...]
    all_gather x8 -> x0, waiting for transfers between devices: 355 us -> none  [the longest x4 186 us: col_gather(): return lax.all_gather(values, 'col', axis=0, tiled=True)]
    pallas_call x0 -> x1, Pallas kernels: none -> 244 us  [run_layer(): pl.pallas_call(layer_kernel, out_shape=[o[0] for o in outs], in_specs=[an...]
    dot_general x26 -> x0, matrix products: 94.1 us -> none  [the longest x4 31.7 us: row_product(): lax.dot_general(gathered, weight, (((1,), (contract,)), ((), ())), prefer...]
    convert_element_type x17 -> x4, other arithmetic: 41.1 us -> 2.93 us  [the longest x1 1.12 us: shards(): fin_u.reshape(256, D).astype(F32)]
    reduce_sum x10 -> x0, other arithmetic: 24.2 us -> none  [the longest x1 4.61 us: grid_plan(): up_bias_grad = jnp.sum(grad_up_g.astype(jnp.float32), 0)]
    psum x6 -> x1, blocking collectives: 54.1 us -> 43.2 us  [shards(): joined = lax.psum(joined, ('dp', 'row', 'col'))]
  transfers between devices with their start and end apart: 17 -> 0, of which waited for: 17 -> 0; matrix products, arithmetic and copies ran while one was open for 4% -> 0% of each run, Pallas kernels for 0% -> 0%
where the time goes in v1:
time: 304 us; the launch traced here: 303 us
  Pallas kernels  244 us (80%)
  blocking collectives  43.2 us (14%)
  local copies, waits for them, and re-layouts  11.9 us (4%)
    pallas_call x1, Pallas kernels, run_layer(): pl.pallas_call(layer_kernel, out_shape=[o[0] for o in outs], in_specs=[an...  244 us
    psum x1, blocking collectives, shards(): joined = lax.psum(joined, ('dp', 'row', 'col'))  43.2 us

profile of v1, /device:TPU:0, one launch (start us, length us, event | category | flops | bytes accessed | tf_op | source)
XLA Modules:
  0.0 303.4 jit_solution(5768896860137436867)
XLA Ops:
  0.7 0.7 copy-done.16
  1.4 0.6 pad.10.seg_in
  2.2 0.7 stack.29.vecs
  2.9 0.3 scatter.9.bias_in
  3.2 1.1 reshape.157
  4.3 0.4 copy.36
  4.7 0.1 reshape.158
  4.8 1.0 copy.37.wq_in
  5.9 244.5 %layer.1 = (bf16[2,512,256]{2,1,0:T(8,128)(2,1)}, f32[2,512,256]{2,1,0:T(8,128)}, bf16[2,128,768]{2,1,0:T(8,128)(2,1)}, bf16[2,2,64,256]{3,2,1,0:T(8,128)(2,1)},...) custom-call(f32[8,512]{1,0:T(8,128)} %pad.10.seg_in, ...), custom_call_target="tpu_custom_call" | custom-call | tf_op jit(solution)/shard_map/layer/pallas_call | solution.py:987
  250.4 0.8 slice.91
  251.3 43.2 %psum.7 = f32[12288]{0:T(1024)S(1)} all-reduce(f32[12288]{0:T(1024)S(1)} %pad_maximum_fusion), channel_id=1, replica_groups=mesh['dp'=2,'row'=4,'col'=4] {'dp','row','col'}, use_global_device_ids=true, to_apply=%region_0.1 | all-reduce | flops 12288 | bytes 98304 | tf_op jit(solution)/shard_map/psum | solution.py:1051
  294.5 0.6 constant_dynamic-slice_fusion.1
  295.1 0.6 dynamic_slice.11
  295.7 0.7 fusion
  296.4 0.7 bitcast_convert_fusion.2
  297.1 0.4 copy.38
  297.6 0.6 reshape.173
  298.2 0.1 copy.39
  298.3 1.1 copy.42
  299.4 1.1 bitcast_convert_fusion.1
  300.6 1.1 bitcast_convert_fusion
  301.6 0.0 copy-done.3
  301.7 0.8 copy.50
  302.5 1.0 copy.51
  (48 shorter events, 0.4 us)
Async XLA Ops:
  0.7 0.7 copy-start.16
  0.7 0.7 copy-start.15
  1.4 0.7 copy-start.13
  1.4 0.7 copy-start.8
  1.4 0.7 copy-start.9
  1.4 0.7 copy-start.10
  1.4 0.7 copy-start.11
  1.4 0.7 copy-start.12
  2.2 0.7 copy-start.14
  3.2 1.1 copy-start.5
  250.4 0.8 copy-start.7
  251.3 45.1 %copy-start.6 = (bf16[2,2,64,256]{3,2,1,0:T(8,128)(2,1)S(1)}, bf16[2,2,64,256]{3,2,1,0:T(8,128)(2,1)}, u32[]{:S(2)}) copy-start(bf16[2,2,64,256]{3,2,1,0:T(8,128)(2,1)} %get-tuple-element.49) | copy-start | bytes 393220
  251.3 45.8 %copy-start.4 = (bf16[2,128,768]{2,1,0:T(8,128)(2,1)S(1)}, bf16[2,128,768]{2,1,0:T(8,128)(2,1)}, u32[]{:S(2)}) copy-start(bf16[2,128,768]{2,1,0:T(8,128)(2,1)} %get-tuple-element.47) | copy-start | bytes 1179652
  298.3 1.2 copy-start.2
  299.4 1.1 copy-start.1
  300.6 1.1 copy-start.3
  300.6 1.9 copy-start

commit v2 on v1

--- a/solution.py
+++ b/solution.py
@@ -55,6 +55,10 @@
     wo,
     wu,
     wd,
+    stage_q,
+    stage_o,
+    stage_u,
+    stage_d,
     proj,
     probs,
     ctx,
@@ -86,13 +90,23 @@
     gup,
     gd,
     xq,
+    xq1,
     xo,
     xu,
     xd,
+    xd1,
     zq,
+    zq1,
     zo,
     zu,
     zd,
+    zd1,
+    vec_sum,
+    vec_rows,
+    vec_out_parts,
+    vec_cols,
+    vec_part,
+    vec_pair,
     ss,
     rs,
     ls,
@@ -186,19 +200,51 @@
     def down_half(ref, half, ci):
         return ref.at[ci, half]
 
+    def qkv_chunk(ref, half, ci, chip):
+        return ref.at[pl.ds(2 * chip, 2), half, :, pl.ds(al(ci, 384), 384)]
+
+    def out_chunk(ref, half, ci, chip):
+        return ref.at[ci, half, :, pl.ds(al(chip, 512), 512)]
+
+    def up_chunk(ref, half, ci, chip):
+        return ref.at[pl.ds(2 * chip, 2), half, :, pl.ds(al(ci, 512), 512)]
+
+    down_chunk = out_chunk
+    far_dev = (d, r, (c + 2) % 4)
+    near_dev = (d, r, c + 1 - 2 * ic)
+
     class Weight:
-        def __init__(self, buffer, piece, place, half):
-            self.buffer, self.piece, self.place, self.half = buffer, piece, place, half
+        def __init__(self, buffer, piece, place, chunk, stage):
+            self.buffer, self.piece, self.place, self.stage = buffer, piece, place, stage
             self.s1, self.r1, self.l1 = new("s", 2), new("r", 4), new("l")
-            self.s2, self.r2 = new("s", 3), new("r", 4)
-            self.s3, self.r3 = new("s", 2), new("r", 2)
+            self.relay_copy = remote(new("s"), self.r1 + r2, stage, place(r2), core_dev)
+            self.staged = remote(self.s1, self.r1 + r2, stage, stage, y_dev)
+            self.ready_waits = []
+            self.far_copy, self.near_copy, self.pair_far, self.pair_near = {}, {}, {}, {}
+            for n in (0, 1):
+                chip = y if n == 0 else 1 - y
+                held = chunk(buffer, p, ic, chip)
+                wanted = chunk(buffer, p, 1 - ic, chip)
+                self.far_copy[n] = remote(new("s"), new("r"), held, held, far_dev)
+                si, ri = new("s"), new("r")
+                self.near_copy[n] = (
+                    remote(si, ri, held, held, near_dev),
+                    remote(si, ri, wanted, wanted, near_dev),
+                )
+                si, ri = new("s"), new("r")
+                missing = chunk(buffer, 1 - p, ic, chip)
+                self.pair_far[n] = (
+                    remote(si, ri, held, held, x_dev),
+                    remote(si, ri, missing, missing, x_dev),
+                )
+                si, ri = new("s"), new("r")
+                missing = chunk(buffer, 1 - p, 1 - ic, chip)
+                self.pair_near[n] = (
+                    remote(si, ri, wanted, wanted, x_dev),
+                    remote(si, ri, missing, missing, x_dev),
+                )
 
         def spread_rows(self):
-            other = remote(
-                self.s1, self.r1 + r, self.piece(1 - y), self.place(r), (d, 2 * (1 - y) + kc, c)
-            )
-            other.start()
-            later(other)
             near = remote(self.s1 + 1, self.r1 + r, self.piece(y), self.place(r), core_dev)
             own = pltpu.make_async_copy(self.piece(y), self.place(r), ls.at[self.l1])
 
@@ -212,55 +258,76 @@
             def _():
                 own.start()
 
-            self.own = own
-
-        def spread_cols(self):
-            copies = []
-            for j in (1, 2, 3):
-                region = self.half(self.buffer, p, ic)
-                copies.append(
-                    remote(self.s2 + j - 1, self.r2 + c, region, region, (d, r, (c + j) % 4))
-                )
+            direct = remote(self.s1, self.r1 + r, self.piece(1 - y), self.place(r), y_dev)
+            staged = remote(self.s1, self.r1 + r, self.piece(1 - y), self.stage, y_dev)
 
             @pl.when(is_agg)
             def _():
-                self.own.wait()
-                for j in (1, 2, 3):
-                    row = (r + j) % 4
-                    remote(
-                        self.s1, self.r1 + row, self.place(row), self.place(row), core_dev
-                    ).wait_recv()
+                direct.start()
+
+            @pl.when(jnp.logical_not(is_agg))
+            def _():
+                staged.start()
+
+            later(direct)
+            self.own = own
+
+        def relay(self):
+            @pl.when(jnp.logical_not(is_agg))
+            def _():
+                self.staged.wait_recv()
+                self.relay_copy.start()
+
+            later(self.relay_copy, jnp.logical_not(is_agg))
+
+        def lead(self, n):
+            copies = (self.far_copy[n], self.near_copy[n][0])
+
+            @pl.when(is_agg)
+            def _():
+                rows = [r1] if n == 0 else [r2, r3]
+                if n == 0:
+                    self.own.wait()
+                for row in rows:
+                    place = self.place(row)
+                    remote(self.s1 + 1, self.r1 + row, place, place, core_dev).wait_recv()
                 for copy in copies:
                     copy.start()
 
             for copy in copies:
                 later(copy, is_agg)
 
-        def spread_pair(self):
-            for ci in (0, 1):
-                source = 2 * k + ci
-                region = self.half(self.buffer, p, ci)
-                copy = remote(self.s3 + ci, self.r3 + ci, region, region, x_dev)
-
-                @pl.when(source != c)
+        def follow(self, n):
+            copies = (self.near_copy[n][0], self.pair_far[n][0])
+            other = jnp.logical_not(is_agg)
+
+            @pl.when(other)
+            def _():
+                self.far_copy[n].wait_recv()
+                for copy in copies:
+                    copy.start()
+
+            for copy in copies:
+                later(copy, other)
+
+        def pair(self, n):
+            self.near_copy[n][1].wait_recv()
+            self.pair_near[n][0].start()
+            later(self.pair_near[n][0])
+
+        def ready(self):
+            for n in (0, 1):
+
+                @pl.when(jnp.logical_not(is_agg))
                 def _():
-                    remote(self.s2, self.r2 + source, region, region, x_dev).wait_recv()
-                    copy.start()
-
-                later(copy, source != c)
-
-        def ready(self):
-            for ci in (0, 1):
-                region = self.half(self.buffer, 1 - p, ci)
-
-                @pl.when(2 * k + ci != c)
-                def _():
-                    remote(self.s3 + ci, self.r3 + ci, region, region, x_dev).wait_recv()
-
-    w_qkv = Weight(wq, qkv_piece, qkv_place, qkv_half)
-    w_out = Weight(wo, out_piece, out_place, out_half)
-    w_up = Weight(wu, up_piece, up_place, up_half)
-    w_down = Weight(wd, down_piece, down_place, down_half)
+                    self.pair_far[n][1].wait_recv()
+
+                self.pair_near[n][1].wait_recv()
+
+    w_qkv = Weight(wq, qkv_piece, qkv_place, qkv_chunk, stage_q)
+    w_out = Weight(wo, out_piece, out_place, out_chunk, stage_o)
+    w_up = Weight(wu, up_piece, up_place, up_chunk, stage_u)
+    w_down = Weight(wd, down_piece, down_place, down_chunk, stage_d)
 
     def rows_of(ref, s, row):
         return ref.at[s, pl.ds(al(row, ROWS), ROWS), :]
@@ -272,37 +339,37 @@
         def __init__(self, full, at, s, source=None):
             self.full, self.at, self.s = full, at, s
             self.source = source
-            self.si, self.ri = new("s", 3), new("r", 3)
+            self.si, self.ri = [new("s"), new("s"), new("s")], new("r", 3)
 
         def send(self):
             mine = self.source if self.source is not None else self.at(self.full, self.s, r)
             place = self.at(self.full, self.s, r)
             for n, dev in ((0, y_dev), (1, core_dev)):
-                copy = remote(self.si + n, self.ri + n, mine, place, dev)
+                copy = remote(self.si[n], self.ri + n, mine, place, dev)
                 copy.start()
                 later(copy)
 
         def forward(self):
             place = self.at(self.full, self.s, r2)
-            remote(self.si, self.ri, place, place, y_dev).wait_recv()
-            copy = remote(self.si + 2, self.ri + 2, place, place, core_dev)
+            remote(self.si[0], self.ri, place, place, y_dev).wait_recv()
+            copy = remote(self.si[2], self.ri + 2, place, place, core_dev)
             copy.start()
             later(copy)
 
         def wait(self):
             near = self.at(self.full, self.s, r1)
-            remote(self.si, self.ri + 1, near, near, core_dev).wait_recv()
+            remote(self.si[1], self.ri + 1, near, near, core_dev).wait_recv()
             far = self.at(self.full, self.s, r3)
-            remote(self.si, self.ri + 2, far, far, core_dev).wait_recv()
+            remote(self.si[2], self.ri + 2, far, far, core_dev).wait_recv()
 
     class Scatter:
         def __init__(self, source, at, core_recv, y_send, y_recv, s):
             self.source, self.at = source, at
             self.core_recv, self.y_send, self.y_recv, self.s = core_recv, y_send, y_recv, s
-            si, ri = new("s", 3), new("r", 3)
-            self.far = remote(si, ri, at(source, s, r3), core_recv.at[s, 1], core_dev)
-            self.near = remote(si + 1, ri + 1, at(source, s, r1), core_recv.at[s, 0], core_dev)
-            self.cross = remote(si + 2, ri + 2, y_send.at[s], y_recv.at[s], y_dev)
+            si, ri = [new("s"), new("s"), new("s")], new("r", 3)
+            self.far = remote(si[0], ri, at(source, s, r3), core_recv.at[s, 1], core_dev)
+            self.near = remote(si[1], ri + 1, at(source, s, r1), core_recv.at[s, 0], core_dev)
+            self.cross = remote(si[2], ri + 2, y_send.at[s], y_recv.at[s], y_dev)
 
         def to_core(self):
             self.far.start()
@@ -351,38 +418,31 @@
         copy.start()
         later(copy)
     biases[c] = bias_in[...]
+    w_out.spread_rows()
     for s in (0, 1):
         x_gather[s].send()
         x_own[s].start()
 
-    w_qkv.spread_cols()
-    w_out.spread_rows()
     w_up.spread_rows()
+    w_down.spread_rows()
+    w_qkv.lead(0)
+    w_qkv.relay()
+    w_out.relay()
+    w_qkv.follow(0)
+    w_qkv.lead(1)
+    w_out.lead(0)
+    w_out.lead(1)
+    w_up.lead(0)
+    w_qkv.pair(0)
+    w_qkv.follow(1)
     x_gather[0].forward()
-    w_qkv.spread_pair()
+    w_out.follow(0)
+    w_qkv.pair(1)
+    w_out.follow(1)
     x_gather[1].forward()
-    w_out.spread_cols()
-    w_up.spread_cols()
-    w_down.spread_rows()
-
-    og_s, og_r, og_l = new("s", 3), new("r", 4), new("l")
-
-    def og_place(row):
-        return og.at[:, :, pl.ds(al(row, 256), 256)]
-
-    og_own = pltpu.make_async_copy(og_in.at[:, pl.ds(al(r, ROWS), ROWS), :], og_place(r), ls.at[og_l])
-    og_own.start()
-    for j in (1, 2, 3):
-        row = (r + j) % 4
-        copy = remote(
-            og_s + j - 1,
-            og_r + r,
-            og_in.at[:, pl.ds(al(row, ROWS), ROWS), :],
-            og_place(r),
-            (d, row, c),
-        )
-        copy.start()
-        later(copy)
+    w_out.pair(0)
+    w_out.pair(1)
+    w_up.relay()
 
     for j in (1, 2, 3):
         source = (c + j) % 4
@@ -399,7 +459,7 @@
     later(seg_copy, r != c)
     w_qkv.ready()
 
-    vec_out[...] = jnp.zeros_like(vec_out)
+    vec_sum[...] = jnp.zeros_like(vec_sum)
 
     def project(s):
         rows = xf[s]
@@ -477,29 +537,57 @@
         hf[s, own_rows, :] = (normed * gain1 + offset1).astype(BF)
         ag1[s].send()
 
-    for s in (0, 1):
-        if s == 0:
-            x_own[0].wait()
-            x_gather[0].wait()
-        else:
-            x_own[1].wait()
-            x_gather[1].wait()
-        project(s)
-        if s == 0:
-            w_out.spread_pair()
-            w_down.spread_cols()
-        attend(s)
-        if s == 0:
-            w_out.ready()
-        else:
-            w_up.spread_pair()
-        out_partial(s)
-        rs1[s].to_core()
-        rs1[s].to_y()
+    og_s, og_r, og_l = new("s", 3), new("r", 4), new("l")
+
+    def og_place(row):
+        return og.at[:, :, pl.ds(al(row, 256), 256)]
+
+    og_own = pltpu.make_async_copy(og_in.at[:, pl.ds(al(r, ROWS), ROWS), :], og_place(r), ls.at[og_l])
+
+    def send_og():
+        og_own.start()
+        for j in (1, 2, 3):
+            row = (r + j) % 4
+            copy = remote(
+                og_s + j - 1,
+                og_r + r,
+                og_in.at[:, pl.ds(al(row, ROWS), ROWS), :],
+                og_place(r),
+                (d, row, c),
+            )
+            copy.start()
+            later(copy)
+
+    x_own[0].wait()
+    x_gather[0].wait()
+    project(0)
+    w_up.lead(1)
+    w_up.follow(0)
+    attend(0)
+    w_out.ready()
+    out_partial(0)
+    rs1[0].to_core()
+    w_down.relay()
+    w_down.lead(0)
+    w_down.lead(1)
+    rs1[0].to_y()
+    x_own[1].wait()
+    x_gather[1].wait()
+    project(1)
+    w_up.follow(1)
+    w_up.pair(0)
+    attend(1)
+    out_partial(1)
+    rs1[1].to_core()
+    rs1[1].to_y()
+    w_down.follow(0)
     first_norm(0)
+    w_up.pair(1)
+    w_down.pair(0)
+    first_norm(1)
+    w_down.follow(1)
     ag1[0].forward()
-    first_norm(1)
-    w_down.spread_pair()
+    w_down.pair(1)
     w_up.ready()
     ag1[0].wait()
 
@@ -538,23 +626,18 @@
     ag2 = [Gather(gdf, rows_of, s) for s in (0, 1)]
     lo_s, lo_r, lo_l = new("s", 6), new("r", 8), new("l", 2)
 
-    og_own.wait()
-    for j in (1, 2, 3):
-        source = (r + j) % 4
-        remote(og_s, og_r + source, og_place(source), og_place(source), core_dev).wait_recv()
-
     def second_norm(s):
         hidden = normed1[s] * gain1 + offset1
         second_sum = rs2[s].result() + down_bias + hidden
         normed, inverse = norm_stats(second_sum)
         lo[s] = (normed * gain2 + offset2).astype(BF)
         grad = og[s].astype(F32)
-        vec_out[0:1, :] += col_sum(grad * normed)
-        vec_out[1:2, :] += col_sum(grad)
+        vec_sum[0:1, :] += col_sum(grad * normed)
+        vec_sum[1:2, :] += col_sum(grad)
         grad_second = norm_pull(grad, normed, inverse, gain2)
         gsec[s] = grad_second
         rounded = grad_second.astype(BF)
-        vec_out[4:5, :] += col_sum(rounded.astype(F32))
+        vec_sum[4:5, :] += col_sum(rounded.astype(F32))
         gdf[s, own_rows, :] = rounded
         ag2[s].send()
 
@@ -578,199 +661,211 @@
             copy.start()
             later(copy)
 
-    for s in (0, 1):
-        if s == 1:
-            ag1[1].wait()
-        mlp_up(s)
-        if s == 0:
-            ag1[1].forward()
-            w_down.ready()
-        rs1[s].sent()
-        mlp_down(s)
-        rs2[s].to_core()
-        rs2[s].to_y()
+    mlp_up(0)
+    ag1[1].forward()
+    send_og()
+    w_down.ready()
+    rs1[0].sent()
+    mlp_down(0)
+    rs2[0].to_core()
+    rs2[0].to_y()
+    ag1[1].wait()
+    mlp_up(1)
+    rs1[1].sent()
+    mlp_down(1)
+    rs2[1].to_core()
+    rs2[1].to_y()
+    og_own.wait()
+    for j in (1, 2, 3):
+        source = (r + j) % 4
+        remote(og_s, og_r + source, og_place(source), og_place(source), core_dev).wait_recv()
+
     second_norm(0)
+    second_norm(1)
     ag2[0].forward()
-    second_norm(1)
     ag2[0].wait()
 
-    def pull_act(s):
-        rows = gdf[s]
-
-        def tile(n, carry):
-            cols = pl.ds(al(n, 256), 256)
-            grad = dot(rows, wd[n // 2, n % 2], 1, 1) * gelup[s, :, cols].astype(F32)
-            rounded = grad.astype(BF)
-            gu[s, :, cols] = rounded
-            vec_out[6:7, cols] += col_sum(rounded.astype(F32))
-            return carry
-
-        lax.fori_loop(0, 4, tile, 0)
-
-    def pull_hidden(s):
-        rows = gu[s]
-
-        def tile(n, carry):
-            weight = wu[n].reshape(256, D)
-            part[s, :, pl.ds(al(n, 256), 256)] = dot(rows, weight, 1, 1).astype(BF)
-            return carry
-
-        lax.fori_loop(0, 4, tile, 0)
-
-    rs3 = scatters()
-    ag3 = [Gather(gaf, rows_of, s) for s in (0, 1)]
-
-    def first_norm_pull(s):
-        grad = gsec[s] + rs3[s].result()
-        normed = normed1[s]
-        vec_out[2:3, :] += col_sum(grad * normed)
-        vec_out[3:4, :] += col_sum(grad)
-        rounded = norm_pull(grad, normed, inv1[s][:, 0:1], gain1).astype(BF)
-        vec_out[5:6, :] += col_sum(rounded.astype(F32))
-        gaf[s, own_rows, :] = rounded
-        ag3[s].send()
-
-    for s in (0, 1):
-        if s == 1:
-            ag2[1].wait()
-        pull_act(s)
-        if s == 0:
-            ag2[1].forward()
-        rs2[s].sent()
-        pull_hidden(s)
-        rs3[s].to_core()
-        rs3[s].to_y()
-        send_lo(s)
-
     class Grad:
-        def __init__(self, buffer, half, pair_half, pair_recv, col_recv, piece, place, fin_half):
-            self.buffer, self.half, self.pair_half = buffer, half, pair_half
-            self.pair_recv, self.col_recv = pair_recv, col_recv
-            self.piece, self.place, self.fin_half = piece, place, fin_half
-            self.s1, self.r1 = new("s"), new("r")
-            self.s2, self.r2 = new("s", 2), new("r", 3)
-            self.s3, self.r3, self.l3 = new("s", 3), new("r", 2), new("l")
-            self.s4, self.r4 = new("s"), new("r")
-            self.pair = remote(
-                self.s1, self.r1, self.pair_half(self.buffer, 1 - p), self.pair_recv, x_dev
-            )
-
-        def to_pair(self):
-            self.pair.start()
-            later(self.pair)
-
-        def to_cols(self):
-            self.pair.wait_recv()
-            mine = self.pair_half(self.buffer, p)
-            mine[...] = (mine[...].astype(F32) + self.pair_recv[...].astype(F32)).astype(BF)
-            for ci in (0, 1):
-                owner = 2 * k + ci
-                slot = (c - owner + 3) % 4
-                copy = remote(
-                    self.s2 + ci,
-                    self.r2 + slot,
-                    self.half(self.buffer, p, ci),
-                    self.col_recv.at[slot],
-                    (d, r, owner),
+        def __init__(self, buffer, chunk, both, by_ci, pair_recv, col_recv, place, pair_first):
+            self.buffer, self.place, self.pair_first = buffer, place, pair_first
+            pair_recvs, col_recvs = pair_recv, col_recv
+            self.near_copy, self.far_copy, self.pair_copy = {}, {}, {}
+            self.near_add, self.far_add, self.pair_add = {}, {}, {}
+            self.own, self.rows_copies = None, {}
+            self.chunk = chunk
+            self.s3, self.r3, self.l3 = new("s", 7), new("r", 4), new("l")
+            for n in (0, 1):
+                chip = y if n == 0 else 1 - y
+                pair_recv, col_recv = pair_recvs[n], col_recvs[n]
+                if pair_first[n]:
+                    pair_src, pair_dst = both(buffer, 1 - p, chip), both(buffer, p, chip)
+                    near_src, held = chunk(buffer, p, 1 - ic, chip), chunk(buffer, p, ic, chip)
+                else:
+                    pair_src, pair_dst = chunk(buffer, 1 - p, ic, chip), chunk(buffer, p, ic, chip)
+                    near_src, held = by_ci(buffer, 1 - ic, chip), by_ci(buffer, ic, chip)
+                self.pair_copy[n] = remote(new("s"), new("r"), pair_src, pair_recv, x_dev)
+                self.near_copy[n] = remote(new("s"), new("r"), near_src, col_recv.at[0], near_dev)
+                self.far_copy[n] = remote(new("s"), new("r"), held, col_recv.at[1], far_dev)
+                self.pair_add[n] = (pair_dst, pair_recv)
+                self.near_add[n] = (held, col_recv.at[0])
+                self.far_add[n] = (held, col_recv.at[1])
+
+        def add(self, refs):
+            mine, other = refs
+            mine[...] = (mine[...].astype(F32) + other[...].astype(F32)).astype(BF)
+
+        def arrival(self, half, yp):
+            return self.r3 + 2 * half + yp
+
+        def rows_of_chunk(self, n):
+            copies = []
+            here, there = d, d + 1 - 2 * p
+            if n == 0:
+                self.own = pltpu.make_async_copy(self.piece(r), self.place(p, y), ls.at[self.l3])
+                targets = [(here, r1), (there, r), (there, r1)]
+                at = 0
+            else:
+                targets = [(here, r2), (there, r2), (here, r3), (there, r3)]
+                at = 3
+            for plane, row in targets:
+                copies.append(
+                    remote(
+                        self.s3 + at,
+                        self.arrival(p, y),
+                        self.piece(row),
+                        self.place(p, y),
+                        (plane, row, c),
+                    )
                 )
-
-                @pl.when(owner != c)
+                at += 1
+            return copies
+
+        def begin(self, n):
+            first = self.pair_copy[n] if self.pair_first[n] else self.near_copy[n]
+            first.start()
+            later(first)
+
+        def second(self, n):
+            if self.pair_first[n]:
+                self.pair_copy[n].wait_recv()
+                self.add(self.pair_add[n])
+                self.near_copy[n].start()
+                later(self.near_copy[n])
+            else:
+                self.near_copy[n].wait_recv()
+                self.add(self.near_add[n])
+
+                @pl.when(jnp.logical_not(is_agg))
                 def _():
-                    copy.start()
-
-                later(copy, owner != c)
-
-        def to_rows(self):
-            own = pltpu.make_async_copy(self.piece(r), self.place(y), ls.at[self.l3])
-            self.own = own
-            copies = []
-            for j in (1, 2, 3):
-                row = (r + j) % 4
-                copies.append(
-                    remote(self.s3 + j - 1, self.r3 + y, self.piece(row), self.place(y), (d, row, c))
-                )
+                    self.far_copy[n].start()
+
+                later(self.far_copy[n], jnp.logical_not(is_agg))
+
+        def third(self, n):
+            if self.pair_first[n]:
+                self.near_copy[n].wait_recv()
+                self.add(self.near_add[n])
+
+                @pl.when(jnp.logical_not(is_agg))
+                def _():
+                    self.far_copy[n].start()
+
+                later(self.far_copy[n], jnp.logical_not(is_agg))
+            else:
+
+                @pl.when(is_agg)
+                def _():
+                    self.far_copy[n].wait_recv()
+                    self.add(self.far_add[n])
+                    self.pair_copy[n].start()
+
+                later(self.pair_copy[n], is_agg)
+
+        def to_rows(self, n):
+            copies = self.rows_of_chunk(n)
 
             @pl.when(is_agg)
             def _():
-                for slot in (0, 1, 2):
-                    dst = self.col_recv.at[slot]
-                    remote(self.s2, self.r2 + slot, dst, dst, core_dev).wait_recv()
-                mine = self.half(self.buffer, p, ic)
-                total = mine[...].astype(F32)
-                for slot in (0, 1, 2):
-                    total = total + self.col_recv[slot].astype(F32)
-                mine[...] = total.astype(BF)
-                own.start()
+                if self.pair_first[n]:
+                    self.far_copy[n].wait_recv()
+                    self.add(self.far_add[n])
+                else:
+                    self.pair_copy[n].wait_recv()
+                    self.add(self.pair_add[n])
+                if n == 0:
+                    self.own.start()
                 for copy in copies:
                     copy.start()
 
             for copy in copies:
                 later(copy, is_agg)
 
-        def to_pair_again(self):
+        def done(self):
             @pl.when(is_agg)
             def _():
                 self.own.wait()
-                place = self.place(1 - y)
-                remote(self.s3, self.r3 + 1 - y, place, place, core_dev).wait_recv()
 
             @pl.when(jnp.logical_not(is_agg))
             def _():
-                for yp in (0, 1):
-                    place = self.place(yp)
-                    remote(self.s3, self.r3 + yp, place, place, core_dev).wait_recv()
-
-            self.last = remote(self.s4, self.r4, self.fin_half(p), self.fin_half(p), x_dev)
-            self.last.start()
-            later(self.last)
-
-        def done(self):
-            dst = self.fin_half(1 - p)
-            remote(self.s4, self.r4, dst, dst, x_dev).wait_recv()
-
-    def lead_half(ref, half):
-        return ref.at[:, half]
+                place = self.place(p, y)
+                remote(self.s3, self.arrival(p, y), place, place, core_dev).wait_recv()
+
+            for half, yp in ((p, 1 - y), (1 - p, y), (1 - p, 1 - y)):
+                place = self.place(half, yp)
+                remote(self.s3, self.arrival(half, yp), place, place, core_dev).wait_recv()
+
+    def rows_both(ref, half, chip):
+        return ref.at[pl.ds(2 * chip, 2), half]
+
+    def cols_both(ref, half, chip):
+        return ref.at[:, half, :, pl.ds(al(chip, 512), 512)]
+
+    def cols_of_ci(ref, ci, chip):
+        return ref.at[ci, :, :, pl.ds(al(chip, 512), 512)]
+
+    def rows_of_ci(ref, ci, chip):
+        return ref.at[pl.ds(2 * chip, 2), :, :, pl.ds(al(ci, 384), 384)]
+
+    def two(ref):
+        return [ref.at[0], ref.at[1]]
 
     g_qkv = Grad(
         gq,
-        qkv_half,
-        lead_half,
-        xq,
-        zq,
-        lambda row: gq.at[row, p, :, pl.ds(al(ic, 384), 384)],
-        lambda yp: fin_q.at[p, :, pl.ds(al(yp, 384), 384)],
-        lambda half: fin_q.at[half],
+        qkv_chunk,
+        rows_both,
+        rows_of_ci,
+        [xq, xq1],
+        [zq, zq1],
+        lambda half, yp: fin_q.at[half, :, pl.ds(al(yp, 384), 384)],
+        (False, True),
     )
+    g_qkv.piece = lambda row: gq.at[row, p, :, pl.ds(al(ic, 384), 384)]
     g_out = Grad(
-        go,
-        out_half,
-        lead_half,
-        xo,
-        zo,
-        lambda row: go.at[ic, p, :, pl.ds(al(row, 256), 256)],
-        lambda yp: fin_o.at[yp, p],
-        lambda half: fin_o.at[:, half],
+        go, out_chunk, cols_both, None, two(xo), two(zo), lambda half, yp: fin_o.at[yp, half], (True, True)
     )
+    g_out.piece = lambda row: go.at[ic, p, :, pl.ds(al(row, 256), 256)]
     g_up = Grad(
         gup,
-        up_half,
-        lead_half,
-        xu,
-        zu,
-        lambda row: gup.at[row, p, :, pl.ds(al(ic, 512), 512)],
-        lambda yp: fin_u.at[p, :, pl.ds(al(yp, 512), 512)],
-        lambda half: fin_u.at[half],
+        up_chunk,
+        rows_both,
+        None,
+        two(xu),
+        two(zu),
+        lambda half, yp: fin_u.at[half, :, pl.ds(al(yp, 512), 512)],
+        (True, True),
     )
+    g_up.piece = lambda row: gup.at[row, p, :, pl.ds(al(ic, 512), 512)]
     g_down = Grad(
         gd,
-        down_half,
-        lead_half,
-        xd,
-        zd,
-        lambda row: gd.at[ic, p, :, pl.ds(al(row, 256), 256)],
-        lambda yp: fin_d.at[yp, p],
-        lambda half: fin_d.at[:, half],
+        down_chunk,
+        cols_both,
+        cols_of_ci,
+        [xd, xd1],
+        [zd, zd1],
+        lambda half, yp: fin_d.at[yp, half],
+        (True, False),
     )
+    g_down.piece = lambda row: gd.at[ic, p, :, pl.ds(al(row, 256), 256)]
 
     def tokens_by(ref, cols):
         return ref[:, :, cols].reshape(2 * SEQ, cols.size)
@@ -807,13 +902,65 @@
 
         lax.fori_loop(0, 4, tile, 0)
 
+    def pull_act(s):
+        rows = gdf[s]
+
+        def tile(n, carry):
+            cols = pl.ds(al(n, 256), 256)
+            grad = dot(rows, wd[n // 2, n % 2], 1, 1) * gelup[s, :, cols].astype(F32)
+            rounded = grad.astype(BF)
+            gu[s, :, cols] = rounded
+            vec_sum[6:7, cols] += col_sum(rounded.astype(F32))
+            return carry
+
+        lax.fori_loop(0, 4, tile, 0)
+
+    def pull_hidden(s):
+        rows = gu[s]
+
+        def tile(n, carry):
+            weight = wu[n].reshape(256, D)
+            part[s, :, pl.ds(al(n, 256), 256)] = dot(rows, weight, 1, 1).astype(BF)
+            return carry
+
+        lax.fori_loop(0, 4, tile, 0)
+
+    rs3 = scatters()
+    ag3 = [Gather(gaf, rows_of, s) for s in (0, 1)]
+
+    def first_norm_pull(s):
+        grad = gsec[s] + rs3[s].result()
+        normed = normed1[s]
+        vec_sum[2:3, :] += col_sum(grad * normed)
+        vec_sum[3:4, :] += col_sum(grad)
+        rounded = norm_pull(grad, normed, inv1[s][:, 0:1], gain1).astype(BF)
+        vec_sum[5:6, :] += col_sum(rounded.astype(F32))
+        gaf[s, own_rows, :] = rounded
+        ag3[s].send()
+
+    pull_act(0)
+    rs2[0].sent()
+    pull_hidden(0)
+    rs3[0].to_core()
+    ag2[1].forward()
+    rs3[0].to_y()
+    ag2[1].wait()
     down_grad()
-    g_down.to_pair()
+    g_down.begin(1)
+    g_down.begin(0)
+    pull_act(1)
+    rs2[1].sent()
+    pull_hidden(1)
+    rs3[1].to_core()
+    rs3[1].to_y()
     first_norm_pull(0)
+    up_grad()
+    g_up.begin(1)
+    g_up.begin(0)
+    g_down.second(1)
+    g_down.second(0)
+    first_norm_pull(1)
     ag3[0].forward()
-    first_norm_pull(1)
-    up_grad()
-    g_up.to_pair()
     ag3[0].wait()
 
     def pull_attend(s):
@@ -847,9 +994,9 @@
             gproj[s, :, columns(ci, 1)] = both_k.astype(BF)
             gproj[s, :, columns(ci, 2)] = both_v
             at = pl.ds(al(ci, 128), 128)
-            vec_out[7:8, at] += col_sum(both_q.astype(F32))
+            vec_sum[7:8, at] += col_sum(both_q.astype(F32))
             at = pl.ds(pl.multiple_of(256 + ci * 128, 128), 128)
-            vec_out[7:8, at] += col_sum(both_v.astype(F32))
+            vec_sum[7:8, at] += col_sum(both_v.astype(F32))
             return carry
 
         lax.fori_loop(0, 2, pair, 0)
@@ -871,34 +1018,113 @@
         tg[s] = rs4[s].result() + slab_of(gaf, s, r)[...].astype(F32)
         tg_copy[s].start()
 
-    for s in (0, 1):
-        if s == 1:
-            ag3[1].wait()
-        pull_attend(s)
-        if s == 0:
-            ag3[1].forward()
-            g_down.to_cols()
-        else:
-            g_up.to_cols()
-        pull_tokens(s)
-        rs4[s].to_core()
-        rs4[s].to_y()
+    class Sums:
+        def __init__(self):
+            self.si, self.ri = new("s", 7), new("r", 9)
+            self.pair = remote(self.si + 6, self.ri + 8, vec_part, vec_pair, x_dev)
+
+        def to_rows(self):
+            vec_rows[r] = vec_sum[...]
+            for j in (1, 2, 3):
+                copy = remote(
+                    self.si + j - 1, self.ri + r, vec_sum, vec_rows.at[r], (d, (r + j) % 4, c)
+                )
+                copy.start()
+                later(copy)
+
+        def to_cols(self):
+            for j in (1, 2, 3):
+                place = vec_rows.at[(r + j) % 4]
+                remote(self.si, self.ri + (r + j) % 4, place, place, core_dev).wait_recv()
+            mine = pl.ds(al(r, 256), 256)
+            features = vec_rows[0, 0:6, mine] + vec_rows[1, 0:6, mine]
+            features = features + vec_rows[2, 0:6, mine] + vec_rows[3, 0:6, mine]
+            for j in (0, 1, 2, 3):
+                to = (c + j) % 4
+                slot = vec_out_parts.at[j]
+                slot[0:6, :] = features
+                for yp in (0, 1):
+                    row = 2 * yp + to // 2
+                    ci = to % 2
+                    for n in (0, 1):
+                        at = pl.ds(pl.multiple_of(ci * 512 + n * 256, 256), 256)
+                        slot[6 + 2 * yp + n : 7 + 2 * yp + n, :] = vec_rows[row, 6:7, at]
+                        at = pl.ds(pl.multiple_of(n * 256 + ci * 128, 128), 128)
+                        slot[10 + n : 11 + n, yp * 128 : yp * 128 + 128] = vec_rows[row, 7:8, at]
+                slot[12:16, :] = jnp.zeros((4, 256), F32)
+                if j > 0:
+                    copy = remote(
+                        self.si + 2 + j,
+                        self.ri + 4 + c,
+                        slot,
+                        vec_cols.at[c],
+                        (d, r, to),
+                    )
+                    copy.start()
+                    later(copy)
+
+        def to_pair(self):
+            total = vec_out_parts[0]
+            for j in (1, 2, 3):
+                source = (c + j) % 4
+                place = vec_cols.at[source]
+                remote(self.si, self.ri + 4 + source, place, place, core_dev).wait_recv()
+                total = total + vec_cols[source]
+            vec_part[...] = total
+            self.pair.start()
+            later(self.pair)
+
+        def done(self):
+            self.pair.wait_recv()
+            vec_out[...] = vec_part[...] + vec_pair[...]
+
+    pull_attend(0)
+    ag3[1].forward()
+    g_up.second(1)
+    pull_tokens(0)
+    rs4[0].to_core()
+    g_down.third(1)
+    rs4[0].to_y()
+    g_down.third(0)
+    ag3[1].wait()
+    pull_attend(1)
     qkv_grad()
-    g_qkv.to_pair()
+    g_qkv.begin(1)
+    g_up.third(1)
     out_grad()
-    g_out.to_pair()
-    g_down.to_rows()
+    g_out.begin(1)
+    g_out.begin(0)
+    g_up.second(0)
+    g_qkv.begin(0)
+    pull_tokens(1)
+    rs4[1].to_core()
+    g_down.to_rows(0)
+    rs4[1].to_y()
+    sums = Sums()
+    sums.to_rows()
+    g_down.to_rows(1)
     tokens_done(0)
-    g_up.to_rows()
-    g_qkv.to_cols()
-    g_out.to_cols()
+    g_up.to_rows(1)
+    sums.to_cols()
+    g_up.third(0)
+    g_qkv.second(1)
+    g_qkv.second(0)
     tokens_done(1)
-    g_down.to_pair_again()
-    g_up.to_pair_again()
-    g_qkv.to_rows()
-    g_out.to_rows()
-    g_qkv.to_pair_again()
-    g_out.to_pair_again()
+    g_out.second(1)
+    g_out.second(0)
+    g_up.to_rows(0)
+    send_lo(0)
+    send_lo(1)
+    g_qkv.third(1)
+    g_out.third(1)
+    g_out.third(0)
+    g_qkv.third(0)
+    g_qkv.to_rows(1)
+    g_out.to_rows(1)
+    g_out.to_rows(0)
+    g_qkv.to_rows(0)
+    sums.to_pair()
+    sums.done()
     for grad in (g_down, g_up, g_qkv, g_out):
         grad.done()
 
@@ -918,8 +1144,8 @@
             pl.when(condition)(copy.wait_send)
 
 
-S_SEMS = 160
-R_SEMS = 160
+S_SEMS = 240
+R_SEMS = 240
 L_SEMS = 32
 
 
@@ -934,7 +1160,7 @@
         (out((2, 2, 64, 256), BF), any_spec),
         (out((2, 128, D), BF), any_spec),
         (out((2, 2, 256, 256), BF), any_spec),
-        (out((8, D), F32), vmem),
+        (out((16, 256), F32), vmem),
     ]
     full = ((2, SEQ, D), BF)
     scratch = [
@@ -945,6 +1171,10 @@
         ((2, 2, 64, D), BF),
         ((4, 2, 128, D), BF),
         ((2, 2, 256, D), BF),
+        ((2, 128, 384), BF),
+        ((2, 64, 256), BF),
+        ((2, 128, 512), BF),
+        ((2, 256, 256), BF),
         ((2, SEQ, 768), BF),
         ((2, 4, SEQ, SEQ), BF),
         ((2, SEQ, 256), BF),
@@ -975,14 +1205,24 @@
         ((2, 2, 64, D), BF),
         ((4, 2, 128, D), BF),
         ((2, 2, 256, D), BF),
-        ((4, 128, 768), BF),
-        ((2, 64, D), BF),
-        ((4, 128, D), BF),
-        ((2, 256, D), BF),
-        ((3, 4, 128, 384), BF),
-        ((3, 64, D), BF),
-        ((3, 4, 128, 512), BF),
-        ((3, 256, D), BF),
+        ((2, 128, 384), BF),
+        ((2, 128, 768), BF),
+        ((2, 2, 64, 512), BF),
+        ((2, 2, 128, D), BF),
+        ((2, 256, 512), BF),
+        ((256, 512), BF),
+        ((2, 2, 2, 128, 384), BF),
+        ((2, 2, 128, 384), BF),
+        ((2, 2, 64, 512), BF),
+        ((2, 2, 2, 128, 512), BF),
+        ((2, 256, 512), BF),
+        ((2, 2, 256, 512), BF),
+        ((8, D), F32),
+        ((4, 8, D), F32),
+        ((4, 16, 256), F32),
+        ((4, 16, 256), F32),
+        ((16, 256), F32),
+        ((16, 256), F32),
     ]
     return pl.pallas_call(
         layer_kernel,
@@ -1020,9 +1260,6 @@
     norm2_bias,
     out_grad,
 ):
-    row = lax.axis_index("row")
-    col = lax.axis_index("col")
-    y, k = row // 2, row % 2
     labels = jnp.pad(segments.astype(F32), ((0, 6), (0, 0)))
     wq = qkv_weight.reshape(256, 3, 2, 128).transpose(0, 2, 1, 3).reshape(2, 128, 768)
     bias = jnp.zeros((8, D), F32)
@@ -1041,37 +1278,26 @@
         bias,
         vecs,
     )
-    up_part = lax.dynamic_update_slice(
-        jnp.zeros((4, 2, 512), F32), vec[6].reshape(2, 1, 512), (2 * k, y, 0)
-    )
-    qv_part = lax.dynamic_update_slice(
-        jnp.zeros((2, 4, 2, 128), F32), vec[7, :512].reshape(2, 2, 1, 128), (0, 2 * k, y, 0)
-    )
-    joined = jnp.concatenate([vec[:6].reshape(-1), up_part.reshape(-1), qv_part.reshape(-1)])
-    joined = lax.psum(joined, ("dp", "row", "col"))
-    features = lax.dynamic_slice_in_dim(joined[: 6 * D].reshape(6, D), row * 256, 256, 1)
-    up_bias_grad = lax.dynamic_slice_in_dim(joined[6 * D : 10 * D], col * D, D)
-    qv_bias_grad = lax.dynamic_slice_in_dim(joined[10 * D :].reshape(2, D), col * 256, 256, 1)
-    grads = (fin_q, fin_o, fin_u, fin_d)
+    grads = (fin_q, fin_o, fin_u, fin_d, vec)
     if pairs is not None:
         grads = lax.psum(grads, "dp", axis_index_groups=pairs)
-    fin_q, fin_o, fin_u, fin_d = grads
+    fin_q, fin_o, fin_u, fin_d, vec = grads
     fin_q = fin_q.reshape(256, 2, 3, 128).transpose(0, 2, 1, 3).reshape(256, 3, 256)
     return (
         lo.reshape(2 * SEQ, 256),
         tg.reshape(2 * SEQ, 256),
         fin_q.astype(F32),
-        qv_bias_grad,
+        vec[10:12],
         fin_o.reshape(256, 256).astype(F32),
-        features[5],
-        features[2],
-        features[3],
+        vec[5],
+        vec[2],
+        vec[3],
         fin_u.reshape(256, D).astype(F32),
-        up_bias_grad,
+        vec[6:10].reshape(D),
         fin_d.reshape(D, 256).astype(F32),
-        features[4],
-        features[0],
-        features[1],
+        vec[4],
+        vec[0],
+        vec[1],
     )
 
 

time: 304 us -> 224 us (0.74)
  blocking collectives: 43.2 us -> 0 us
  Pallas kernels: 244 us -> 206 us
    psum x1 -> x0, blocking collectives: 43.2 us -> none  [shards(): joined = lax.psum(joined, ('dp', 'row', 'col'))]
    pallas_call x1, Pallas kernels: 244 us -> 206 us  [run_layer(): pl.pallas_call(layer_kernel, out_shape=[o[0] for o in outs], in_specs=[an...]
where the time goes in v2:
time: 224 us
  Pallas kernels  206 us (92%)
  local copies, waits for them, and re-layouts  13.3 us (6%)
  other arithmetic  3.82 us (2%)
    pallas_call x1, Pallas kernels, run_layer(): pl.pallas_call(layer_kernel, out_shape=[o[0] for o in outs], in_specs=[an...  206 us
    unnamed x36, local copies, waits for them, and re-layouts  5.11 us

profile of v2, /device:TPU:0, one launch (start us, length us, event | category | flops | bytes accessed | tf_op | source)
XLA Modules:
  0.0 223.7 jit_solution(9511127087678751505)
XLA Ops:
  0.7 0.7 copy-done.14
  1.4 0.6 pad.10.seg_in
  2.1 0.0 copy-done.9
  2.1 0.7 stack.29.vecs
  2.8 0.3 scatter.9.bias_in
  3.1 1.1 reshape.133
  4.3 0.4 copy.34
  4.7 0.1 reshape.134
  4.8 1.0 copy.35.wq_in
  5.8 205.7 %layer.1 = (bf16[2,512,256]{2,1,0:T(8,128)(2,1)}, f32[2,512,256]{2,1,0:T(8,128)}, bf16[2,128,768]{2,1,0:T(8,128)(2,1)}, bf16[2,2,64,256]{3,2,1,0:T(8,128)(2,1)},...) custom-call(f32[8,512]{1,0:T(8,128)} %pad.10.seg_in, ...), custom_call_target="tpu_custom_call" | custom-call | tf_op jit(solution)/shard_map/layer/pallas_call | solution.py:1227
  211.6 1.3 slice.57
  212.9 0.7 slice_bitcast_fusion
  213.6 1.5 fusion
  215.1 0.6 copy.40
  215.7 1.6 bitcast_convert_fusion.2
  217.4 0.4 copy.36
  217.8 0.6 reshape.147
  218.4 0.1 copy.37
  218.5 1.1 copy.38
  219.7 1.1 bitcast_convert_fusion.1
  220.8 1.1 bitcast_convert_fusion
  221.9 0.0 copy-done.3
  221.9 0.8 copy.44
  222.7 1.0 copy.45
  (30 shorter events, 0.2 us)
Async XLA Ops:
  0.6 0.7 copy-start.14
  0.7 0.7 copy-start.13
  1.4 0.7 copy-start.11
  1.4 0.7 copy-start.6
  1.4 0.7 copy-start.7
  1.4 0.7 copy-start.8
  1.4 0.7 copy-start.9
  1.4 0.7 copy-start.10
  2.1 0.7 copy-start.12
  3.1 1.1 copy-start.5
  211.6 5.8 %copy-start.4 = (bf16[2,128,768]{2,1,0:T(8,128)(2,1)S(1)}, bf16[2,128,768]{2,1,0:T(8,128)(2,1)}, u32[]{:S(2)}) copy-start(bf16[2,128,768]{2,1,0:T(8,128)(2,1)} %get-tuple-element.47) | copy-start | bytes 1179652
  218.5 1.2 copy-start.2
  219.7 1.1 copy-start.1
  220.8 1.1 copy-start.3
  220.8 1.9 copy-start

commit v3 on v2

--- a/solution.py
+++ b/solution.py
@@ -39,8 +39,14 @@
     wo_in,
     wu_in,
     wd_in,
-    bias_in,
-    vecs,
+    up_bias_in,
+    qv_bias_in,
+    out_bias_in,
+    gain1_in,
+    offset1_in,
+    down_bias_in,
+    gain2_in,
+    offset2_in,
     lo_out,
     tg_out,
     fin_q,
@@ -49,6 +55,7 @@
     fin_d,
     vec_out,
     seg,
+    bias_own,
     biases,
     xf,
     wq,
@@ -73,6 +80,7 @@
     act,
     gelup,
     og,
+    og_stage,
     lo,
     gsec,
     gdf,
@@ -164,28 +172,28 @@
     def _():
         pl.semaphore_wait(barrier, 7)
 
-    def qkv_piece(yp):
-        return wq_in.at[:, :, pl.ds(al(yp, 384), 384)]
-
-    def out_piece(yp):
+    def qkv_piece(yp, n):
+        return wq_in.at[n, :, :, pl.ds(al(yp, 128), 128)]
+
+    def out_piece(yp, n):
         return wo_in.at[yp]
 
-    def up_piece(yp):
+    def up_piece(yp, n):
         return wu_in.at[:, :, pl.ds(al(yp, 512), 512)]
 
-    def down_piece(yp):
+    def down_piece(yp, n):
         return wd_in.at[yp]
 
-    def qkv_place(row):
-        return wq.at[row, :, :, pl.ds(al(ic, 384), 384)]
-
-    def out_place(row):
+    def qkv_place(row, n):
+        return wq.at[row, :, :, pl.ds(pl.multiple_of(ic * 384 + n * 128, 128), 128)]
+
+    def out_place(row, n):
         return wo.at[ic, :, :, pl.ds(al(row, 256), 256)]
 
-    def up_place(row):
+    def up_place(row, n):
         return wu.at[row, :, :, pl.ds(al(ic, 512), 512)]
 
-    def down_place(row):
+    def down_place(row, n):
         return wd.at[ic, :, :, pl.ds(al(row, 256), 256)]
 
     def qkv_half(ref, half, ci):
@@ -214,12 +222,19 @@
     near_dev = (d, r, c + 1 - 2 * ic)
 
     class Weight:
-        def __init__(self, buffer, piece, place, chunk, stage):
-            self.buffer, self.piece, self.place, self.stage = buffer, piece, place, stage
-            self.s1, self.r1, self.l1 = new("s", 2), new("r", 4), new("l")
-            self.relay_copy = remote(new("s"), self.r1 + r2, stage, place(r2), core_dev)
-            self.staged = remote(self.s1, self.r1 + r2, stage, stage, y_dev)
-            self.ready_waits = []
+        def __init__(self, buffer, piece, place, chunk, stages):
+            self.piece, self.place, self.stages = piece, place, stages
+            self.parts = range(len(stages))
+            self.s1, self.r1, self.l1 = [], [], []
+            self.relay_copies, self.staged = [], []
+            for q, stage in enumerate(stages):
+                self.s1.append(new("s", 2))
+                self.r1.append(new("r", 4))
+                self.l1.append(new("l"))
+                self.relay_copies.append(
+                    remote(new("s"), self.r1[q] + r2, stage, place(r2, q), core_dev)
+                )
+                self.staged.append(remote(self.s1[q], self.r1[q] + r2, stage, stage, y_dev))
             self.far_copy, self.near_copy, self.pair_far, self.pair_near = {}, {}, {}, {}
             for n in (0, 1):
                 chip = y if n == 0 else 1 - y
@@ -245,40 +260,38 @@
                 )
 
         def spread_rows(self):
-            near = remote(self.s1 + 1, self.r1 + r, self.piece(y), self.place(r), core_dev)
-            own = pltpu.make_async_copy(self.piece(y), self.place(r), ls.at[self.l1])
-
-            @pl.when(jnp.logical_not(is_agg))
-            def _():
-                near.start()
-
-            later(near, jnp.logical_not(is_agg))
-
-            @pl.when(is_agg)
-            def _():
-                own.start()
-
-            direct = remote(self.s1, self.r1 + r, self.piece(1 - y), self.place(r), y_dev)
-            staged = remote(self.s1, self.r1 + r, self.piece(1 - y), self.stage, y_dev)
-
-            @pl.when(is_agg)
-            def _():
-                direct.start()
-
-            @pl.when(jnp.logical_not(is_agg))
-            def _():
-                staged.start()
-
-            later(direct)
-            self.own = own
+            self.own = []
+            for q in self.parts:
+                mine, to = self.piece(y, q), self.place(r, q)
+                across = self.piece(1 - y, q)
+                near = remote(self.s1[q] + 1, self.r1[q] + r, mine, to, core_dev)
+                own = pltpu.make_async_copy(mine, to, ls.at[self.l1[q]])
+                direct = remote(self.s1[q], self.r1[q] + r, across, to, y_dev)
+                staged = remote(self.s1[q], self.r1[q] + r, across, self.stages[q], y_dev)
+
+                @pl.when(jnp.logical_not(is_agg))
+                def _():
+                    near.start()
+                    staged.start()
+
+                @pl.when(is_agg)
+                def _():
+                    own.start()
+                    direct.start()
+
+                later(near, jnp.logical_not(is_agg))
+                later(direct)
+                self.own.append(own)
 
         def relay(self):
             @pl.when(jnp.logical_not(is_agg))
             def _():
-                self.staged.wait_recv()
-                self.relay_copy.start()
-
-            later(self.relay_copy, jnp.logical_not(is_agg))
+                for q in self.parts:
+                    self.staged[q].wait_recv()
+                    self.relay_copies[q].start()
+
+            for copy in self.relay_copies:
+                later(copy, jnp.logical_not(is_agg))
 
         def lead(self, n):
             copies = (self.far_copy[n], self.near_copy[n][0])
@@ -286,11 +299,12 @@
             @pl.when(is_agg)
             def _():
                 rows = [r1] if n == 0 else [r2, r3]
-                if n == 0:
-                    self.own.wait()
-                for row in rows:
-                    place = self.place(row)
-                    remote(self.s1 + 1, self.r1 + row, place, place, core_dev).wait_recv()
+                for q in self.parts:
+                    if n == 0:
+                        self.own[q].wait()
+                    for row in rows:
+                        place = self.place(row, q)
+                        remote(self.s1[q], self.r1[q] + row, place, place, core_dev).wait_recv()
                 for copy in copies:
                     copy.start()
 
@@ -324,10 +338,10 @@
 
                 self.pair_near[n][1].wait_recv()
 
-    w_qkv = Weight(wq, qkv_piece, qkv_place, qkv_chunk, stage_q)
-    w_out = Weight(wo, out_piece, out_place, out_chunk, stage_o)
-    w_up = Weight(wu, up_piece, up_place, up_chunk, stage_u)
-    w_down = Weight(wd, down_piece, down_place, down_chunk, stage_d)
+    w_qkv = Weight(wq, qkv_piece, qkv_place, qkv_chunk, [stage_q.at[q] for q in (0, 1, 2)])
+    w_out = Weight(wo, out_piece, out_place, out_chunk, [stage_o])
+    w_up = Weight(wu, up_piece, up_place, up_chunk, [stage_u])
+    w_down = Weight(wd, down_piece, down_place, down_chunk, [stage_d])
 
     def rows_of(ref, s, row):
         return ref.at[s, pl.ds(al(row, ROWS), ROWS), :]
@@ -411,13 +425,15 @@
         seg_own.start()
 
     bias_s, bias_r = new("s", 3), new("r", 4)
+    bias_own[...] = jnp.zeros_like(bias_own)
+    bias_own[0:1, :] = up_bias_in[...]
+    bias_own[1:2, 0:256] = qv_bias_in[0:1, :]
+    bias_own[1:2, 256:512] = qv_bias_in[1:2, :]
     for j in (1, 2, 3):
-        copy = remote(
-            bias_s + j - 1, bias_r + c, bias_in, biases.at[c], (d, r, (c + j) % 4)
-        )
+        copy = remote(bias_s + j - 1, bias_r + c, bias_own, biases.at[c], (d, r, (c + j) % 4))
         copy.start()
         later(copy)
-    biases[c] = bias_in[...]
+    biases[c] = bias_own[...]
     w_out.spread_rows()
     for s in (0, 1):
         x_gather[s].send()
@@ -425,6 +441,37 @@
 
     w_up.spread_rows()
     w_down.spread_rows()
+    og_s, og_r, og_l = new("s", 4), new("r", 5), new("l")
+
+    def og_place(row):
+        return og.at[:, :, pl.ds(al(row, 256), 256)]
+
+    def og_rows(row):
+        return og_in.at[:, pl.ds(al(row, ROWS), ROWS), :]
+
+    og_own = pltpu.make_async_copy(og_rows(r), og_place(r), ls.at[og_l])
+    og_own.start()
+    og_copies = [
+        remote(og_s, og_r + r, og_rows(r1), og_place(r), core_dev),
+        remote(og_s + 1, og_r + r, og_rows(r2), og_place(r), y_dev),
+        remote(og_s + 2, og_r + 4, og_rows(r3), og_stage, y_dev),
+    ]
+    for copy in og_copies:
+        copy.start()
+        later(copy)
+    og_relay = remote(og_s + 3, og_r + r2, og_stage, og_place(r2), core_dev)
+
+    def relay_og():
+        remote(og_s + 2, og_r + 4, og_stage, og_stage, y_dev).wait_recv()
+        og_relay.start()
+        later(og_relay)
+
+    def wait_og():
+        og_own.wait()
+        for j in (1, 2, 3):
+            place = og_place((r + j) % 4)
+            remote(og_s, og_r + (r + j) % 4, place, place, core_dev).wait_recv()
+
     w_qkv.lead(0)
     w_qkv.relay()
     w_out.relay()
@@ -478,7 +525,7 @@
         return pl.ds(pl.multiple_of(ci * 384 + n * 128, 128), 128)
 
     def attend(s):
-        labels = seg[s : s + 1, :]
+        labels = seg[s : s + 1, :].astype(F32)
         down = jnp.transpose(jnp.broadcast_to(labels, (128, SEQ)))[:, 0:1]
         mask[...] = jnp.where(down == labels, 0.0, -1e30)
         lane = lax.broadcasted_iota(jnp.int32, (SEQ, 128), 1)
@@ -519,8 +566,8 @@
         second = jnp.sum(scaled * normed, 1, keepdims=True) * (1.0 / D)
         return inverse * (scaled - first - normed * second)
 
-    out_bias, gain1, offset1 = vecs[0:1, :], vecs[1:2, :], vecs[2:3, :]
-    down_bias, gain2, offset2 = vecs[3:4, :], vecs[4:5, :], vecs[5:6, :]
+    out_bias, gain1, offset1 = out_bias_in[...], gain1_in[...], offset1_in[...]
+    down_bias, gain2, offset2 = down_bias_in[...], gain2_in[...], offset2_in[...]
     own_rows = pl.ds(al(r, ROWS), ROWS)
 
     def scatters():
@@ -536,27 +583,6 @@
         inv1[s] = jnp.broadcast_to(inverse, (ROWS, 128))
         hf[s, own_rows, :] = (normed * gain1 + offset1).astype(BF)
         ag1[s].send()
-
-    og_s, og_r, og_l = new("s", 3), new("r", 4), new("l")
-
-    def og_place(row):
-        return og.at[:, :, pl.ds(al(row, 256), 256)]
-
-    og_own = pltpu.make_async_copy(og_in.at[:, pl.ds(al(r, ROWS), ROWS), :], og_place(r), ls.at[og_l])
-
-    def send_og():
-        og_own.start()
-        for j in (1, 2, 3):
-            row = (r + j) % 4
-            copy = remote(
-                og_s + j - 1,
-                og_r + r,
-                og_in.at[:, pl.ds(al(row, ROWS), ROWS), :],
-                og_place(r),
-                (d, row, c),
-            )
-            copy.start()
-            later(copy)
 
     x_own[0].wait()
     x_gather[0].wait()
@@ -575,19 +601,19 @@
     x_gather[1].wait()
     project(1)
     w_up.follow(1)
-    w_up.pair(0)
     attend(1)
     out_partial(1)
     rs1[1].to_core()
     rs1[1].to_y()
+    w_up.pair(0)
     w_down.follow(0)
     first_norm(0)
     w_up.pair(1)
+    w_down.follow(1)
     w_down.pair(0)
     first_norm(1)
-    w_down.follow(1)
+    w_down.pair(1)
     ag1[0].forward()
-    w_down.pair(1)
     w_up.ready()
     ag1[0].wait()
 
@@ -663,7 +689,7 @@
 
     mlp_up(0)
     ag1[1].forward()
-    send_og()
+    relay_og()
     w_down.ready()
     rs1[0].sent()
     mlp_down(0)
@@ -675,11 +701,7 @@
     mlp_down(1)
     rs2[1].to_core()
     rs2[1].to_y()
-    og_own.wait()
-    for j in (1, 2, 3):
-        source = (r + j) % 4
-        remote(og_s, og_r + source, og_place(source), og_place(source), core_dev).wait_recv()
-
+    wait_og()
     second_norm(0)
     second_norm(1)
     ag2[0].forward()
@@ -1088,6 +1110,8 @@
     g_down.third(0)
     ag3[1].wait()
     pull_attend(1)
+    sums = Sums()
+    sums.to_rows()
     qkv_grad()
     g_qkv.begin(1)
     g_up.third(1)
@@ -1100,8 +1124,6 @@
     rs4[1].to_core()
     g_down.to_rows(0)
     rs4[1].to_y()
-    sums = Sums()
-    sums.to_rows()
     g_down.to_rows(1)
     tokens_done(0)
     g_up.to_rows(1)
@@ -1149,7 +1171,7 @@
 L_SEMS = 32
 
 
-def run_layer(seg, x, og, wq, wo, wu, wd, bias, vecs):
+def run_layer(seg, x, og, wq, wo, wu, wd, *vecs):
     any_spec = pl.BlockSpec(memory_space=pl.ANY)
     vmem = pl.BlockSpec(memory_space=pltpu.VMEM)
     out = jax.ShapeDtypeStruct
@@ -1164,14 +1186,15 @@
     ]
     full = ((2, SEQ, D), BF)
     scratch = [
-        ((8, SEQ), F32),
+        ((2, SEQ), jnp.int32),
+        ((8, D), F32),
         ((4, 8, D), F32),
         full,
         ((4, 2, 128, 768), BF),
         ((2, 2, 64, D), BF),
         ((4, 2, 128, D), BF),
         ((2, 2, 256, D), BF),
-        ((2, 128, 384), BF),
+        ((3, 2, 128, 128), BF),
         ((2, 64, 256), BF),
         ((2, 128, 512), BF),
         ((2, 256, 256), BF),
@@ -1189,6 +1212,7 @@
         full,
         full,
         ((2, ROWS, D), BF),
+        ((2, ROWS, 256), BF),
         ((2, ROWS, D), BF),
         ((2, ROWS, D), F32),
         full,
@@ -1227,7 +1251,7 @@
     return pl.pallas_call(
         layer_kernel,
         out_shape=[o[0] for o in outs],
-        in_specs=[any_spec] * 7 + [vmem] * 2,
+        in_specs=[any_spec] * 7 + [vmem] * len(vecs),
         out_specs=[o[1] for o in outs],
         scratch_shapes=[pltpu.VMEM(shape, dtype) for shape, dtype in scratch]
         + [
@@ -1239,7 +1263,49 @@
             collective_id=0, has_side_effects=True, vmem_limit_bytes=62 * 1024 * 1024
         ),
         name="layer",
-    )(seg, x, og, wq, wo, wu, wd, bias, vecs)
+    )(seg, x, og, wq, wo, wu, wd, *vecs)
+
+
+def finish_kernel(lo, tg, fq, fo, fu, fd, vec, lo_out, tg_out, q_out, o_out, u_out, d_out, *vectors):
+    lo_out[...] = lo[...]
+    tg_out[...] = tg[...]
+    for yp in (0, 1):
+        for n in (0, 1, 2):
+            at = yp * 384 + n * 128
+            q_out[n, :, yp * 128 : yp * 128 + 128] = fq[:, at : at + 128].astype(F32)
+    o_out[...] = fo[...].astype(F32)
+    u_out[...] = fu[...].astype(F32)
+    d_out[...] = fd[...].astype(F32)
+    for n in range(6):
+        vectors[n][...] = vec[n : n + 1, :]
+    for n in range(4):
+        vectors[6][:, n * 256 : n * 256 + 256] = vec[6 + n : 7 + n, :]
+    vectors[7][...] = vec[10:12, :]
+
+
+def finish(*arrays):
+    steps = 4
+    out = jax.ShapeDtypeStruct
+
+    def rows_spec(shape):
+        return pl.BlockSpec((shape[0] // steps, shape[1]), lambda i: (i, 0))
+
+    def whole(shape):
+        return pl.BlockSpec(shape, lambda i: (0, 0))
+
+    shapes = [out(arrays[0].shape, BF)] + [out(a.shape, F32) for a in arrays[1:6]]
+    vectors = [out((1, 256), F32)] * 6 + [out((1, D), F32), out((2, 256), F32)]
+    shapes[2] = out((3, 256, 256), F32)
+    out_specs = [rows_spec(a.shape) for a in shapes] + [whole(v.shape) for v in vectors]
+    out_specs[2] = pl.BlockSpec((3, 256 // steps, 256), lambda i: (0, i, 0))
+    return pl.pallas_call(
+        finish_kernel,
+        grid=(steps,),
+        in_specs=[rows_spec(a.shape) for a in arrays[:6]] + [whole(arrays[6].shape)],
+        out_specs=out_specs,
+        out_shape=shapes + vectors,
+        name="finish",
+    )(*arrays)
 
 
 def shards(
@@ -1260,44 +1326,53 @@
     norm2_bias,
     out_grad,
 ):
-    labels = jnp.pad(segments.astype(F32), ((0, 6), (0, 0)))
-    wq = qkv_weight.reshape(256, 3, 2, 128).transpose(0, 2, 1, 3).reshape(2, 128, 768)
-    bias = jnp.zeros((8, D), F32)
-    bias = bias.at[0].set(up_bias).at[1, :512].set(qv_bias.reshape(512))
-    vecs = jnp.stack(
-        [out_bias, norm1_gain, norm1_bias, down_bias, norm2_gain, norm2_bias, out_bias, out_bias]
-    )
     lo, tg, fin_q, fin_o, fin_u, fin_d, vec = run_layer(
-        labels,
+        segments,
         tokens.reshape(2, SEQ, 256),
         out_grad.reshape(2, SEQ, 256),
-        wq,
+        qkv_weight.transpose(1, 0, 2).reshape(3, 2, 128, 256),
         out_weight.reshape(2, 2, 64, 256),
         up_weight.reshape(2, 128, D),
         down_weight.reshape(2, 2, 256, 256),
-        bias,
-        vecs,
+        up_bias.reshape(1, D),
+        qv_bias,
+        out_bias.reshape(1, D),
+        norm1_gain.reshape(1, D),
+        norm1_bias.reshape(1, D),
+        down_bias.reshape(1, D),
+        norm2_gain.reshape(1, D),
+        norm2_bias.reshape(1, D),
     )
     grads = (fin_q, fin_o, fin_u, fin_d, vec)
     if pairs is not None:
         grads = lax.psum(grads, "dp", axis_index_groups=pairs)
     fin_q, fin_o, fin_u, fin_d, vec = grads
-    fin_q = fin_q.reshape(256, 2, 3, 128).transpose(0, 2, 1, 3).reshape(256, 3, 256)
-    return (
+    results = finish(
         lo.reshape(2 * SEQ, 256),
         tg.reshape(2 * SEQ, 256),
-        fin_q.astype(F32),
-        vec[10:12],
-        fin_o.reshape(256, 256).astype(F32),
-        vec[5],
-        vec[2],
-        vec[3],
-        fin_u.reshape(256, D).astype(F32),
-        vec[6:10].reshape(D),
-        fin_d.reshape(D, 256).astype(F32),
-        vec[4],
-        vec[0],
-        vec[1],
+        fin_q.reshape(256, 768),
+        fin_o.reshape(256, 256),
+        fin_u.reshape(256, D),
+        fin_d.reshape(D, 256),
+        vec,
+    )
+    layer_out, tokens_grad, qkv_grad, out_grad_w, up_grad, down_grad = results[:6]
+    n2_gain, n2_bias, n1_gain, n1_bias, down_b, out_b, up_b, qv_b = results[6:]
+    return (
+        layer_out,
+        tokens_grad,
+        qkv_grad.transpose(1, 0, 2),
+        qv_b,
+        out_grad_w,
+        out_b.reshape(256),
+        n1_gain.reshape(256),
+        n1_bias.reshape(256),
+        up_grad,
+        up_b.reshape(D),
+        down_grad,
+        down_b.reshape(256),
+        n2_gain.reshape(256),
+        n2_bias.reshape(256),
     )
 
 

time: 224 us -> 207 us (0.924)
  local copies, waits for them, and re-layouts: 13.3 us -> 0 us
  other arithmetic: 3.82 us -> 0 us
    unnamed x36 -> x0, local copies, waits for them, and re-layouts: 5.11 us -> none
    pallas_call x0 -> x1, Pallas kernels: none -> 4.6 us  [finish(): pl.pallas_call(finish_kernel, grid=(steps,), in_specs=[rows_spec(a.shape)...]
    pallas_call x1, Pallas kernels: 206 us -> 201 us  [run_layer(): pl.pallas_call(layer_kernel, out_shape=[o[0] for o in outs], in_specs=[an...]
    convert_element_type x4 -> x0, other arithmetic: 3.82 us -> none  [the longest x1 1.62 us: shards(): fin_o.reshape(256, 256).astype(F32)]
    slice x2 -> x0, local copies, waits for them, and re-layouts: 2.83 us -> none  [the longest x1 1.5 us: shards(): vec[1]]
    reshape x4 -> x0, local copies, waits for them, and re-layouts: 2.68 us -> none  [shards(): qkv_weight.reshape(256, 3, 2, 128).transpose(0, 2, 1, 3)]
where the time goes in v3:
time: 207 us
  Pallas kernels  206 us (100%)
    pallas_call x1, Pallas kernels, run_layer(): pl.pallas_call(layer_kernel, out_shape=[o[0] for o in outs], in_specs=[an...  201 us
    pallas_call x1, Pallas kernels, finish(): pl.pallas_call(finish_kernel, grid=(steps,), in_specs=[rows_spec(a.shape)...  4.6 us

profile of v3, /device:TPU:0, one launch (start us, length us, event | category | flops | bytes accessed | tf_op | source)
XLA Modules:
  0.0 206.6 jit_solution(18331790173627962291)
XLA Ops:
  0.7 201.1 %layer.1 = (bf16[2,512,256]{2,1,0:T(8,128)(2,1)}, f32[2,512,256]{2,1,0:T(8,128)}, bf16[2,128,768]{2,1,0:T(8,128)(2,1)}, bf16[2,2,64,256]{3,2,1,0:T(8,128)(2,1)},...) custom-call(s32[2,512]{1,0:T(2,128)} %seg_in.1, ...), custom_call_target="tpu_custom_call" | custom-call | tf_op jit(solution)/shard_map/layer/pallas_call | solution.py:1251
  201.8 4.6 %finish.1 = (bf16[1024,256]{1,0:T(8,128)(2,1)}, f32[1024,256]{1,0:T(8,128)}, f32[3,256,256]{2,1,0:T(8,128)}, f32[256,256]{1,0:T(8,128)}, f32[256,1024]{1,0:T(8,1...) custom-call(bf16[1024,256]{1,0:T(8,128)(2,1)} %bitcast.34, ...), custom_call_target="tpu_custom_call" | custom-call | tf_op jit(solution)/shard_map/finish/pallas_call | solution.py:1301

commit v4 on v3

--- a/solution.py
+++ b/solution.py
@@ -98,13 +98,11 @@
     gup,
     gd,
     xq,
-    xq1,
     xo,
     xu,
     xd,
     xd1,
     zq,
-    zq1,
     zo,
     zu,
     zd,
@@ -208,9 +206,6 @@
     def down_half(ref, half, ci):
         return ref.at[ci, half]
 
-    def qkv_chunk(ref, half, ci, chip):
-        return ref.at[pl.ds(2 * chip, 2), half, :, pl.ds(al(ci, 384), 384)]
-
     def out_chunk(ref, half, ci, chip):
         return ref.at[ci, half, :, pl.ds(al(chip, 512), 512)]
 
@@ -218,11 +213,23 @@
         return ref.at[pl.ds(2 * chip, 2), half, :, pl.ds(al(ci, 512), 512)]
 
     down_chunk = out_chunk
+
+    def qkv_row(ref, half, ci, row):
+        return ref.at[row, half, :, pl.ds(al(ci, 384), 384)]
+
+    def out_row(ref, half, ci, row):
+        return ref.at[ci, half, :, pl.ds(al(row, 256), 256)]
+
+    def up_row(ref, half, ci, row):
+        return ref.at[row, half, :, pl.ds(al(ci, 512), 512)]
+
+    down_row = out_row
+    chip_rows = ((r, r1), (r2, r3))
     far_dev = (d, r, (c + 2) % 4)
     near_dev = (d, r, c + 1 - 2 * ic)
 
     class Weight:
-        def __init__(self, buffer, piece, place, chunk, stages):
+        def __init__(self, buffer, piece, place, at_row, stages):
             self.piece, self.place, self.stages = piece, place, stages
             self.parts = range(len(stages))
             self.s1, self.r1, self.l1 = [], [], []
@@ -236,25 +243,25 @@
                 )
                 self.staged.append(remote(self.s1[q], self.r1[q] + r2, stage, stage, y_dev))
             self.far_copy, self.near_copy, self.pair_far, self.pair_near = {}, {}, {}, {}
-            for n in (0, 1):
-                chip = y if n == 0 else 1 - y
-                held = chunk(buffer, p, ic, chip)
-                wanted = chunk(buffer, p, 1 - ic, chip)
-                self.far_copy[n] = remote(new("s"), new("r"), held, held, far_dev)
+            for n, m in ((0, 0), (0, 1), (1, 0), (1, 1)):
+                row = chip_rows[n][m]
+                held = at_row(buffer, p, ic, row)
+                wanted = at_row(buffer, p, 1 - ic, row)
+                self.far_copy[n, m] = remote(new("s"), new("r"), held, held, far_dev)
                 si, ri = new("s"), new("r")
-                self.near_copy[n] = (
+                self.near_copy[n, m] = (
                     remote(si, ri, held, held, near_dev),
                     remote(si, ri, wanted, wanted, near_dev),
                 )
                 si, ri = new("s"), new("r")
-                missing = chunk(buffer, 1 - p, ic, chip)
-                self.pair_far[n] = (
+                missing = at_row(buffer, 1 - p, ic, row)
+                self.pair_far[n, m] = (
                     remote(si, ri, held, held, x_dev),
                     remote(si, ri, missing, missing, x_dev),
                 )
                 si, ri = new("s"), new("r")
-                missing = chunk(buffer, 1 - p, 1 - ic, chip)
-                self.pair_near[n] = (
+                missing = at_row(buffer, 1 - p, 1 - ic, row)
+                self.pair_near[n, m] = (
                     remote(si, ri, wanted, wanted, x_dev),
                     remote(si, ri, missing, missing, x_dev),
                 )
@@ -294,54 +301,58 @@
                 later(copy, jnp.logical_not(is_agg))
 
         def lead(self, n):
-            copies = (self.far_copy[n], self.near_copy[n][0])
-
             @pl.when(is_agg)
             def _():
-                rows = [r1] if n == 0 else [r2, r3]
-                for q in self.parts:
-                    if n == 0:
-                        self.own[q].wait()
-                    for row in rows:
-                        place = self.place(row, q)
-                        remote(self.s1[q], self.r1[q] + row, place, place, core_dev).wait_recv()
-                for copy in copies:
-                    copy.start()
-
-            for copy in copies:
-                later(copy, is_agg)
+                for m in (0, 1):
+                    row = chip_rows[n][m]
+                    for q in self.parts:
+                        if (n, m) == (0, 0):
+                            self.own[q].wait()
+                        else:
+                            place = self.place(row, q)
+                            remote(
+                                self.s1[q], self.r1[q] + row, place, place, core_dev
+                            ).wait_recv()
+                    self.far_copy[n, m].start()
+                    self.near_copy[n, m][0].start()
+
+            for m in (0, 1):
+                later(self.far_copy[n, m], is_agg)
+                later(self.near_copy[n, m][0], is_agg)
 
         def follow(self, n):
-            copies = (self.near_copy[n][0], self.pair_far[n][0])
             other = jnp.logical_not(is_agg)
 
             @pl.when(other)
             def _():
-                self.far_copy[n].wait_recv()
-                for copy in copies:
-                    copy.start()
-
-            for copy in copies:
-                later(copy, other)
+                for m in (0, 1):
+                    self.far_copy[n, m].wait_recv()
+                    self.near_copy[n, m][0].start()
+                    self.pair_far[n, m][0].start()
+
+            for m in (0, 1):
+                later(self.near_copy[n, m][0], other)
+                later(self.pair_far[n, m][0], other)
 
         def pair(self, n):
-            self.near_copy[n][1].wait_recv()
-            self.pair_near[n][0].start()
-            later(self.pair_near[n][0])
+            for m in (0, 1):
+                self.near_copy[n, m][1].wait_recv()
+                self.pair_near[n, m][0].start()
+                later(self.pair_near[n, m][0])
 
         def ready(self):
-            for n in (0, 1):
+            for key in ((0, 0), (0, 1), (1, 0), (1, 1)):
 
                 @pl.when(jnp.logical_not(is_agg))
                 def _():
-                    self.pair_far[n][1].wait_recv()
-
-                self.pair_near[n][1].wait_recv()
-
-    w_qkv = Weight(wq, qkv_piece, qkv_place, qkv_chunk, [stage_q.at[q] for q in (0, 1, 2)])
-    w_out = Weight(wo, out_piece, out_place, out_chunk, [stage_o])
-    w_up = Weight(wu, up_piece, up_place, up_chunk, [stage_u])
-    w_down = Weight(wd, down_piece, down_place, down_chunk, [stage_d])
+                    self.pair_far[key][1].wait_recv()
+
+                self.pair_near[key][1].wait_recv()
+
+    w_qkv = Weight(wq, qkv_piece, qkv_place, qkv_row, [stage_q.at[q] for q in (0, 1, 2)])
+    w_out = Weight(wo, out_piece, out_place, out_row, [stage_o])
+    w_up = Weight(wu, up_piece, up_place, up_row, [stage_u])
+    w_down = Weight(wd, down_piece, down_place, down_row, [stage_d])
 
     def rows_of(ref, s, row):
         return ref.at[s, pl.ds(al(row, ROWS), ROWS), :]
@@ -595,11 +606,11 @@
     rs1[0].to_core()
     w_down.relay()
     w_down.lead(0)
-    w_down.lead(1)
     rs1[0].to_y()
     x_own[1].wait()
     x_gather[1].wait()
     project(1)
+    w_down.lead(1)
     w_up.follow(1)
     attend(1)
     out_partial(1)
@@ -690,14 +701,14 @@
     mlp_up(0)
     ag1[1].forward()
     relay_og()
+    ag1[1].wait()
+    mlp_up(1)
     w_down.ready()
     rs1[0].sent()
     mlp_down(0)
     rs2[0].to_core()
+    rs1[1].sent()
     rs2[0].to_y()
-    ag1[1].wait()
-    mlp_up(1)
-    rs1[1].sent()
     mlp_down(1)
     rs2[1].to_core()
     rs2[1].to_y()
@@ -708,16 +719,20 @@
     ag2[0].wait()
 
     class Grad:
-        def __init__(self, buffer, chunk, both, by_ci, pair_recv, col_recv, place, pair_first):
+        def __init__(
+            self, buffer, chunk, both, by_ci, pair_recv, col_recv, place, pair_first, by_row=False
+        ):
             self.buffer, self.place, self.pair_first = buffer, place, pair_first
             pair_recvs, col_recvs = pair_recv, col_recv
+            self.by_row = by_row
+            self.rows = (r, r1, r2, r3)
             self.near_copy, self.far_copy, self.pair_copy = {}, {}, {}
             self.near_add, self.far_add, self.pair_add = {}, {}, {}
             self.own, self.rows_copies = None, {}
             self.chunk = chunk
             self.s3, self.r3, self.l3 = new("s", 7), new("r", 4), new("l")
-            for n in (0, 1):
-                chip = y if n == 0 else 1 - y
+            for n in range(len(pair_recv)):
+                chip = self.rows[n] if by_row else (y if n == 0 else 1 - y)
                 pair_recv, col_recv = pair_recvs[n], col_recvs[n]
                 if pair_first[n]:
                     pair_src, pair_dst = both(buffer, 1 - p, chip), both(buffer, p, chip)
@@ -744,6 +759,12 @@
             here, there = d, d + 1 - 2 * p
             if n == 0:
                 self.own = pltpu.make_async_copy(self.piece(r), self.place(p, y), ls.at[self.l3])
+            if self.by_row:
+                targets = [(here, self.rows[n]), (there, self.rows[n])]
+                at = 2 * n - 1
+                if n == 0:
+                    targets, at = targets[1:], 0
+            elif n == 0:
                 targets = [(here, r1), (there, r), (there, r1)]
                 at = 0
             else:
@@ -845,21 +866,22 @@
     def cols_of_ci(ref, ci, chip):
         return ref.at[ci, :, :, pl.ds(al(chip, 512), 512)]
 
-    def rows_of_ci(ref, ci, chip):
-        return ref.at[pl.ds(2 * chip, 2), :, :, pl.ds(al(ci, 384), 384)]
-
     def two(ref):
         return [ref.at[0], ref.at[1]]
 
+    def qkv_row_both(ref, half, row):
+        return ref.at[row, half]
+
     g_qkv = Grad(
         gq,
-        qkv_chunk,
-        rows_both,
-        rows_of_ci,
-        [xq, xq1],
-        [zq, zq1],
+        qkv_row,
+        qkv_row_both,
+        None,
+        [xq.at[n] for n in range(4)],
+        [zq.at[n] for n in range(4)],
         lambda half, yp: fin_q.at[half, :, pl.ds(al(yp, 384), 384)],
-        (False, True),
+        (True,) * 4,
+        by_row=True,
     )
     g_qkv.piece = lambda row: gq.at[row, p, :, pl.ds(al(ic, 384), 384)]
     g_out = Grad(
@@ -892,10 +914,13 @@
     def tokens_by(ref, cols):
         return ref[:, :, cols].reshape(2 * SEQ, cols.size)
 
-    def down_grad():
+    def down_grad(m):
+        cols = pl.ds(al(y if m == 0 else 1 - y, 512), 512)
+
         def tile(n, carry):
             left = tokens_by(act, pl.ds(al(n, 256), 256))
-            gd[n // 2, n % 2] = dot(left, gdf[...].reshape(2 * SEQ, D), 0, 0).astype(BF)
+            right = gdf[:, :, cols].reshape(2 * SEQ, 512)
+            gd[n // 2, n % 2, :, cols] = dot(left, right, 0, 0).astype(BF)
             return carry
 
         lax.fori_loop(0, 4, tile, 0)
@@ -967,9 +992,10 @@
     ag2[1].forward()
     rs3[0].to_y()
     ag2[1].wait()
-    down_grad()
+    down_grad(0)
+    g_down.begin(0)
+    down_grad(1)
     g_down.begin(1)
-    g_down.begin(0)
     pull_act(1)
     rs2[1].sent()
     pull_hidden(1)
@@ -1113,42 +1139,52 @@
     sums = Sums()
     sums.to_rows()
     qkv_grad()
+    g_qkv.begin(3)
+    g_qkv.begin(2)
     g_qkv.begin(1)
-    g_up.third(1)
+    g_up.second(0)
     out_grad()
     g_out.begin(1)
     g_out.begin(0)
-    g_up.second(0)
     g_qkv.begin(0)
+    g_up.third(1)
     pull_tokens(1)
     rs4[1].to_core()
     g_down.to_rows(0)
     rs4[1].to_y()
+    send_lo(0)
+    send_lo(1)
     g_down.to_rows(1)
     tokens_done(0)
+    g_qkv.second(3)
+    sums.to_cols()
     g_up.to_rows(1)
-    sums.to_cols()
+    g_qkv.second(2)
     g_up.third(0)
+    tokens_done(1)
+    g_qkv.third(3)
     g_qkv.second(1)
+    g_qkv.third(2)
+    g_qkv.to_rows(3)
+    g_up.to_rows(0)
+    g_out.second(1)
+    sums.to_pair()
+    g_qkv.third(1)
+    g_qkv.to_rows(2)
+    g_out.second(0)
     g_qkv.second(0)
-    tokens_done(1)
-    g_out.second(1)
-    g_out.second(0)
-    g_up.to_rows(0)
-    send_lo(0)
-    send_lo(1)
-    g_qkv.third(1)
     g_out.third(1)
+    g_qkv.to_rows(1)
     g_out.third(0)
     g_qkv.third(0)
-    g_qkv.to_rows(1)
     g_out.to_rows(1)
     g_out.to_rows(0)
     g_qkv.to_rows(0)
-    sums.to_pair()
     sums.done()
-    for grad in (g_down, g_up, g_qkv, g_out):
-        grad.done()
+    g_down.done()
+    g_up.done()
+    g_out.done()
+    g_qkv.done()
 
     for s in (0, 1):
         rs3[s].sent()
@@ -1166,8 +1202,8 @@
             pl.when(condition)(copy.wait_send)
 
 
-S_SEMS = 240
-R_SEMS = 240
+S_SEMS = 320
+R_SEMS = 320
 L_SEMS = 32
 
 
@@ -1229,14 +1265,12 @@
         ((2, 2, 64, D), BF),
         ((4, 2, 128, D), BF),
         ((2, 2, 256, D), BF),
-        ((2, 128, 384), BF),
-        ((2, 128, 768), BF),
+        ((4, 128, 768), BF),
         ((2, 2, 64, 512), BF),
         ((2, 2, 128, D), BF),
         ((2, 256, 512), BF),
         ((256, 512), BF),
-        ((2, 2, 2, 128, 384), BF),
-        ((2, 2, 128, 384), BF),
+        ((4, 2, 128, 384), BF),
         ((2, 2, 64, 512), BF),
         ((2, 2, 2, 128, 512), BF),
         ((2, 256, 512), BF),
@@ -1284,7 +1318,7 @@
 
 
 def finish(*arrays):
-    steps = 4
+    steps = 2
     out = jax.ShapeDtypeStruct
 
     def rows_spec(shape):

time: 207 us -> 197 us (0.952)
  Pallas kernels: 206 us -> 196 us
    pallas_call x1, Pallas kernels: 201 us -> 193 us  [run_layer(): pl.pallas_call(layer_kernel, out_shape=[o[0] for o in outs], in_specs=[an...]
where the time goes in v4:
time: 197 us
  Pallas kernels  196 us (99%)
    pallas_call x1, Pallas kernels, run_layer(): pl.pallas_call(layer_kernel, out_shape=[o[0] for o in outs], in_specs=[an...  193 us

profile of v4, /device:TPU:0, one launch (start us, length us, event | category | flops | bytes accessed | tf_op | source)
XLA Modules:
  0.0 197.3 jit_solution(13317308107237377821)
XLA Ops:
  0.7 192.7 %layer.1 = (bf16[2,512,256]{2,1,0:T(8,128)(2,1)}, f32[2,512,256]{2,1,0:T(8,128)}, bf16[2,128,768]{2,1,0:T(8,128)(2,1)}, bf16[2,2,64,256]{3,2,1,0:T(8,128)(2,1)},...) custom-call(s32[2,512]{1,0:T(2,128)} %seg_in.1, ...), custom_call_target="tpu_custom_call" | custom-call | tf_op jit(solution)/shard_map/layer/pallas_call | solution.py:1285
  193.3 3.8 %finish.1 = (bf16[1024,256]{1,0:T(8,128)(2,1)}, f32[1024,256]{1,0:T(8,128)}, f32[3,256,256]{2,1,0:T(8,128)}, f32[256,256]{1,0:T(8,128)}, f32[256,1024]{1,0:T(8,1...) custom-call(bf16[1024,256]{1,0:T(8,128)(2,1)} %bitcast.34, ...), custom_call_target="tpu_custom_call" | custom-call | tf_op jit(solution)/shard_map/finish/pallas_call | solution.py:1335

commit v5 on v4

--- a/solution.py
+++ b/solution.py
@@ -334,11 +334,17 @@
                 later(self.near_copy[n, m][0], other)
                 later(self.pair_far[n, m][0], other)
 
-        def pair(self, n):
+        def pair(self, n, spreading):
+            mine = is_agg if spreading else jnp.logical_not(is_agg)
+
+            @pl.when(mine)
+            def _():
+                for m in (0, 1):
+                    self.near_copy[n, m][1].wait_recv()
+                    self.pair_near[n, m][0].start()
+
             for m in (0, 1):
-                self.near_copy[n, m][1].wait_recv()
-                self.pair_near[n, m][0].start()
-                later(self.pair_near[n, m][0])
+                later(self.pair_near[n, m][0], mine)
 
         def ready(self):
             for key in ((0, 0), (0, 1), (1, 0), (1, 1)):
@@ -491,15 +497,19 @@
     w_out.lead(0)
     w_out.lead(1)
     w_up.lead(0)
-    w_qkv.pair(0)
+    w_qkv.pair(0, True)
+    w_qkv.pair(0, False)
     w_qkv.follow(1)
     x_gather[0].forward()
     w_out.follow(0)
-    w_qkv.pair(1)
+    w_qkv.pair(1, True)
+    w_qkv.pair(1, False)
     w_out.follow(1)
     x_gather[1].forward()
-    w_out.pair(0)
-    w_out.pair(1)
+    w_out.pair(0, True)
+    w_out.pair(0, False)
+    w_out.pair(1, True)
+    w_out.pair(1, False)
     w_up.relay()
 
     for j in (1, 2, 3):
@@ -601,6 +611,7 @@
     w_up.lead(1)
     w_up.follow(0)
     attend(0)
+    w_up.pair(0, True)
     w_out.ready()
     out_partial(0)
     rs1[0].to_core()
@@ -613,17 +624,20 @@
     w_down.lead(1)
     w_up.follow(1)
     attend(1)
+    w_up.pair(1, True)
     out_partial(1)
     rs1[1].to_core()
     rs1[1].to_y()
-    w_up.pair(0)
+    w_up.pair(0, False)
+    w_down.pair(0, True)
     w_down.follow(0)
     first_norm(0)
-    w_up.pair(1)
+    w_up.pair(1, False)
     w_down.follow(1)
-    w_down.pair(0)
+    w_down.pair(0, False)
     first_norm(1)
-    w_down.pair(1)
+    w_down.pair(1, True)
+    w_down.pair(1, False)
     ag1[0].forward()
     w_up.ready()
     ag1[0].wait()

time: 197 us -> 193 us (0.980)
  Pallas kernels: 196 us -> 192 us
    pallas_call x1, Pallas kernels: 193 us -> 188 us  [run_layer(): pl.pallas_call(layer_kernel, out_shape=[o[0] for o in outs], in_specs=[an...]
where the time goes in v5:
time: 193 us
  Pallas kernels  192 us (99%)
    pallas_call x1, Pallas kernels, run_layer(): pl.pallas_call(layer_kernel, out_shape=[o[0] for o in outs], in_specs=[an...  188 us

profile of v5, /device:TPU:0, one launch (start us, length us, event | category | flops | bytes accessed | tf_op | source)
XLA Modules:
  0.0 192.9 jit_solution(10727111005193066028)
XLA Ops:
  0.7 188.3 %layer.1 = (bf16[2,512,256]{2,1,0:T(8,128)(2,1)}, f32[2,512,256]{2,1,0:T(8,128)}, bf16[2,128,768]{2,1,0:T(8,128)(2,1)}, bf16[2,2,64,256]{3,2,1,0:T(8,128)(2,1)},...) custom-call(s32[2,512]{1,0:T(2,128)} %seg_in.1, ...), custom_call_target="tpu_custom_call" | custom-call | tf_op jit(solution)/shard_map/layer/pallas_call | solution.py:1299
  189.0 3.8 %finish.1 = (bf16[1024,256]{1,0:T(8,128)(2,1)}, f32[1024,256]{1,0:T(8,128)}, f32[3,256,256]{2,1,0:T(8,128)}, f32[256,256]{1,0:T(8,128)}, f32[256,1024]{1,0:T(8,1...) custom-call(bf16[1024,256]{1,0:T(8,128)(2,1)} %bitcast.34, ...), custom_call_target="tpu_custom_call" | custom-call | tf_op jit(solution)/shard_map/finish/pallas_call | solution.py:1349

commit v6 on v5

--- a/solution.py
+++ b/solution.py
@@ -610,8 +610,8 @@
     project(0)
     w_up.lead(1)
     w_up.follow(0)
+    w_up.pair(0, True)
     attend(0)
-    w_up.pair(0, True)
     w_out.ready()
     out_partial(0)
     rs1[0].to_core()

time: 193 us -> 193 us (level)
  no operation moved by 1% of the time
where the time goes in v6:
time: 193 us
  Pallas kernels  192 us (99%)
    pallas_call x1, Pallas kernels, run_layer(): pl.pallas_call(layer_kernel, out_shape=[o[0] for o in outs], in_specs=[an...  188 us

profile of v6, /device:TPU:0, one launch (start us, length us, event | category | flops | bytes accessed | tf_op | source)
XLA Modules:
  0.0 192.9 jit_solution(7655104302090648080)
XLA Ops:
  0.7 188.3 %layer.1 = (bf16[2,512,256]{2,1,0:T(8,128)(2,1)}, f32[2,512,256]{2,1,0:T(8,128)}, bf16[2,128,768]{2,1,0:T(8,128)(2,1)}, bf16[2,2,64,256]{3,2,1,0:T(8,128)(2,1)},...) custom-call(s32[2,512]{1,0:T(2,128)} %seg_in.1, ...), custom_call_target="tpu_custom_call" | custom-call | tf_op jit(solution)/shard_map/layer/pallas_call | solution.py:1299
  188.9 3.8 %finish.1 = (bf16[1024,256]{1,0:T(8,128)(2,1)}, f32[1024,256]{1,0:T(8,128)}, f32[3,256,256]{2,1,0:T(8,128)}, f32[256,256]{1,0:T(8,128)}, f32[256,1024]{1,0:T(8,1...) custom-call(bf16[1024,256]{1,0:T(8,128)(2,1)} %bitcast.34, ...), custom_call_target="tpu_custom_call" | custom-call | tf_op jit(solution)/shard_map/finish/pallas_call | solution.py:1349
